TPU v7x, 512 devices: a whole 4x8x8 slice. The times are simulated.
512 devices in a mesh: grp: 32 (over x, z), harm: 16 (over y, core).
Axes of the slice: x: 4, y: 8, z: 8, core: 2. Of those that a mesh axis runs over, the one named last changes fastest.
Arguments:
- initial_coef: float32 [64, 16384], P('harm', 'grp'), may hold values from -4 to 4
- load_coef: float32 [64, 16384], P('harm', 'grp'), may hold values from -24 to 24
- mass: float32 [16384], P('grp'), may hold values from 0.5 to 2
- stiffness: float32 [128, 3, 128, 128], P('grp'), may hold values from -0.012 to 12, as said below
- block_offset: int32 [128, 2], P('grp'), may hold values from -2 to 2, as said below
- joint_dofs: int32 [32, 512], P('grp'), may hold values from 0 to 511, each once within a row
- joint_owner: int32 [32, 256], P('grp'), may hold values from 0 to 31, as said below
- elem_stiff: float32 [32, 16, 768], P('grp'), may hold values from 0.03 to 0.3
- slip_force: float32 [32, 16, 768], P('grp'), may hold values from 0.05 to 1
Outputs:
- solution: float32 [64, 16384], P('harm', 'grp')
- residual: float32 [64, 16384], P('harm', 'grp')
Inputs may be any that keep to these rules, and one draw needn't show every extreme that they name: Each diagonal entry of a block stiffness[i, 0] lies between 8 and 12, every other entry between -0.012 and 0.012. `block_offset`: column 0 is -1 or -2, column 1 is 1 or 2. `joint_dofs`: each row is a permutation of 0 to 511. `joint_owner`: among the joints of one row at most 24 have the same owner, and one owner has exactly 24 joints of every row.
All inputs are finite; a program needn't handle non-finite values.
Results may differ from a plain program's by a relative error of at most 0.0003.
Values sent between devices are 32-bit elements; how exact they have to be, the bound alone decides.
A program may use at most 64 MiB of HBM per device.

v0:
```python
import math

import jax
import jax.numpy as jnp
from jax import lax
from jax.sharding import PartitionSpec as P

HARM = 32
NEWTON = 2


highest = lax.Precision.HIGHEST
omega_base = 0.03125
big_force = 1e30


def from_behind(block, axis, distance):
    devices = range(lax.axis_size(axis))
    route = [((i - distance) % len(devices), i) for i in devices]
    return lax.ppermute(block, axis, route)


def entering(array, axis, combine, identity):
    length, index = (lax.axis_size(axis), lax.axis_index(axis))
    everything = jax.tree.map(lambda part: lax.all_gather(part, axis), array)
    start = jax.tree.map(
        lambda part, zero: jnp.broadcast_to(jnp.asarray(zero, part.dtype), part.shape),
        array,
        identity,
    )

    def turn(k, before):
        reached = k < index
        new = combine(before, jax.tree.map(lambda part: part[k], everything))
        return jax.tree.map(lambda a, b: jnp.where(reached, a, b), new, before)

    return lax.fori_loop(0, length, turn, start)


def extended(block, sides, width):
    for axis, dim in sides:
        count = lax.axis_size(axis)
        forward = [(i, i + 1) for i in range(count - 1)]
        backward = [(target, source) for source, target in forward]
        low = lax.ppermute(
            lax.slice_in_dim(block, block.shape[dim] - width, None, axis=dim), axis, forward
        )
        high = lax.ppermute(lax.slice_in_dim(block, 0, width, axis=dim), axis, backward)
        block = jnp.concatenate([low, block, high], axis=dim)
    return block


def harmonic_of(coefs, harmonics):
    return jnp.where(coefs <= harmonics, coefs, coefs - harmonics)


def fourier_basis(times, coefs, harmonics, samples):
    freq = harmonic_of(coefs, harmonics)
    phase = times[:, None] * freq[None, :] % samples
    angle = phase.astype(jnp.float32) * (2.0 * math.pi / samples)
    return jnp.where((coefs > harmonics)[None, :], jnp.sin(angle), jnp.cos(angle))


def coef_weights(coefs, samples):
    return jnp.where(coefs == 0, 1.0 / samples, 2.0 / samples).astype(jnp.float32)


def run_elements(force_start, movement, k_joint, s_joint):

    def advance(force, move_row):
        force = jnp.clip(force + k_joint * move_row[None, :], -s_joint, s_joint)
        return (force, jnp.sum(force, axis=0))

    _, totals = lax.scan(advance, force_start, movement)
    return totals


def combine_maps(earlier, later):
    return (
        earlier[0] + later[0],
        jnp.clip(earlier[1] + later[0], later[1], later[2]),
        jnp.clip(earlier[2] + later[0], later[1], later[2]),
    )


def chain_forces(relative, k_joint, s_joint):
    time_dev = relative.shape[0]
    last_row = from_behind(relative[time_dev - 1], "harm", 1)
    movement = relative - jnp.concatenate([last_row[None, :], relative[:-1]], axis=0)
    neutral = (
        jnp.zeros_like(k_joint),
        jnp.full_like(k_joint, -big_force),
        jnp.full_like(k_joint, big_force),
    )

    def compose(maps, move_row):
        step_map = (k_joint * move_row[None, :], -s_joint, s_joint)
        return (combine_maps(maps, step_map), None)

    local_map, _ = lax.scan(compose, neutral, movement)
    incoming = entering(local_map, "harm", combine_maps, neutral)
    force_start = jnp.clip(incoming[0], incoming[1], incoming[2])
    return run_elements(force_start, movement, k_joint, s_joint)


def local(
    initial_coef,
    load_coef,
    mass,
    stiffness,
    block_offset,
    joint_dofs,
    joint_owner,
    elem_stiff,
    slip_force,
):
    groups = lax.axis_size("grp")
    harm_parts = lax.axis_size("harm")
    harm_index = lax.axis_index("harm")
    samples = 4 * HARM
    coef_dev = initial_coef.shape[0]
    time_dev = samples // harm_parts
    block_count = stiffness.shape[0]
    block_size = stiffness.shape[2]
    dof_dev = block_count * block_size
    joint_dev = dof_dev // 2
    slot_count = elem_stiff.shape[2]
    capacity = slot_count // groups
    my_coefs = harm_index * coef_dev + jnp.arange(coef_dev, dtype=jnp.int32)
    my_times = harm_index * time_dev + jnp.arange(time_dev, dtype=jnp.int32)
    freq = harmonic_of(my_coefs, HARM).astype(jnp.float32) * omega_base
    dynamic = (freq * freq)[:, None] * mass[None, :]
    kdiag = jnp.diagonal(stiffness[:, 0], axis1=1, axis2=2).reshape(dof_dev)
    precond = 1.0 / (kdiag[None, :] - dynamic)
    ordering = joint_dofs[0]
    side_a = ordering[:joint_dev]
    side_b = ordering[joint_dev:]
    position = jnp.arange(dof_dev, dtype=jnp.int32)
    dof_joint = jnp.zeros((dof_dev,), jnp.int32).at[ordering].set(position % joint_dev)
    dof_sign = (
        jnp.zeros((dof_dev,), jnp.float32)
        .at[ordering]
        .set(jnp.where(position < joint_dev, 1.0, -1.0).astype(jnp.float32))
    )
    owners = joint_owner[0]
    onehot = (owners[:, None] == jnp.arange(groups, dtype=jnp.int32)[None, :]).astype(jnp.int32)
    rank = jnp.sum((jnp.cumsum(onehot, axis=0) - onehot) * onehot, axis=1)
    column = owners * capacity + rank
    k_joint = elem_stiff[0]
    s_joint = slip_force[0]
    offsets = jnp.concatenate([jnp.zeros((block_count, 1), jnp.int32), block_offset], axis=1)
    block_index = jnp.arange(block_count, dtype=jnp.int32)[:, None] + 2 + offsets
    current = initial_coef
    latest = load_coef
    for step in range(NEWTON):
        coef_field = current
        padded = extended(coef_field, (("grp", 1),), 2 * block_size)
        blocks = padded.reshape(coef_dev, block_count + 4, block_size)
        taken = blocks[:, block_index, :]
        stiff_part = jnp.einsum("ikrs,ciks->cir", stiffness, taken, precision=highest).reshape(
            coef_dev, dof_dev
        )
        rows = jnp.arange(time_dev * lax.axis_size("harm"), dtype=jnp.int32)
        disp_time = lax.psum_scatter(
            jnp.dot(fourier_basis(rows, my_coefs, HARM, samples), coef_field, precision=highest),
            "harm",
            scatter_dimension=0,
            tiled=True,
        )
        row_count = disp_time.shape[0]
        relative = disp_time[:, side_a] - disp_time[:, side_b]
        outgoing = jnp.zeros((row_count, slot_count), jnp.float32).at[:, column].set(relative)
        arrived = lax.all_to_all(
            outgoing.reshape(row_count, groups, capacity),
            "grp",
            split_axis=1,
            concat_axis=1,
            tiled=True,
        )
        owner_total = chain_forces(arrived.reshape(row_count, slot_count), k_joint, s_joint)
        returned = lax.all_to_all(
            owner_total.reshape(row_count, groups, capacity),
            "grp",
            split_axis=1,
            concat_axis=1,
            tiled=True,
        )
        joint_total = returned.reshape(row_count, slot_count)[:, column]
        force_time = joint_total[:, dof_joint] * dof_sign[None, :]
        coef_rows = jnp.arange(coef_dev * lax.axis_size("harm"), dtype=jnp.int32)
        projector = (
            fourier_basis(my_times, coef_rows, HARM, samples).T
            * coef_weights(coef_rows, samples)[:, None]
        )
        nonlinear = lax.psum_scatter(
            jnp.dot(projector, force_time, precision=highest),
            "harm",
            scatter_dimension=0,
            tiled=True,
        )
        latest = stiff_part - dynamic * coef_field + nonlinear - load_coef
        current = current - precond * latest
    return (current, latest)


def solution(mesh):
    in_specs = (
        P("harm", "grp"),
        P("harm", "grp"),
        P("grp"),
        P("grp", None, None, None),
        P("grp", None),
        P("grp", None),
        P("grp", None),
        P("grp", None, None),
        P("grp", None, None),
    )
    out_specs = (P("harm", "grp"), P("harm", "grp"))
    return jax.shard_map(local, mesh=mesh, in_specs=in_specs, out_specs=out_specs, check_vma=False)
```

profile of v0, /device:TPU:1, one launch (start us, length us, event | category | flops | bytes accessed | tf_op | source)
XLA Modules:
  0.0 615.6 jit_solution(18154099566457232208)
XLA Ops:
  10.0 4.8 collective-permute-start
  19.8 2.4 scatter_custom_fusion.1
  24.7 48.2 %reduce-scatter.3.cloned.1.call-done = f32[8,512]{1,0:T(8,128)} async-done(((f32[128,512]{1,0:T(8,128)}), f32[8,512]{1,0:T(8,128)}) %reduce-scatter.3.cloned.1.call-update) | async-done | bytes 16400 | tf_op jit(solution)/shard_map/reduce_scatter | solution.py:164
  73.7 2.8 scatter_custom_fusion
  77.4 8.9 %all-to-all-start = ((f32[32,1,192]{2,1,0:T(1,128)}), f32[32,1,192]{2,1,0:T(1,128)S(1)}, u32[]{:S(2)}, u32[]{:S(2)}) async-start(f32[32,1,192]{2,1,0:T(1,128)} %reshape.430), calls=%async_computation.1 | async-start | bytes 65536 | tf_op jit(solution)/shard_map/all_to_all | solution.py:173
  86.4 8.8 %all-to-all-done = f32[32,1,192]{2,1,0:T(1,128)S(1)} async-done(((f32[32,1,192]{2,1,0:T(1,128)}), f32[32,1,192]{2,1,0:T(1,128)S(1)}, u32[]{:S(2)}, u32[]{:S(2)}) %all-to-all-start) | async-done | bytes 24608 | tf_op jit(solution)/shard_map/all_to_all | solution.py:173
  96.6 2.9 collective-permute-start.2
  99.9 2.2 collective-permute-done.2
  102.1 7.3 %while.96 = (s32[]{:T(128)}, f32[16,768]{1,0:T(8,128)S(1)}, f32[16,768]{1,0:T(8,128)S(1)}, f32[16,768]{1,0:T(8,128)S(1)}, f32[8,768]{1,0:T(8,128)S(1)}, /*index=...) while((s32[]{:T(128)}, f32[16,768]{1,0:T(8,128)S(1)}, ...), condition=%wide.region_6.7_spmd.clone, body=%wide.region_5.6_spmd.clone.sunk | while | flops 135171 | bytes 451699 | solution.py:100
  109.4 20.3 %all-gather = f32[256,768]{1,0:T(8,128)S(1)} all-gather(f32[16,768]{1,0:T(8,128)S(1)} %get-tuple-element.550), channel_id=2, replica_groups=mesh['grp'=32,'harm'=16] {'harm'}, dimensions={0}, use_global_device_ids=true | all-gather | bytes 835584 | tf_op jit(solution)/shard_map/all_gather | solution.py:25
  129.7 17.7 %all-gather.1 = f32[256,768]{1,0:T(8,128)S(1)} all-gather(f32[16,768]{1,0:T(8,128)S(1)} %get-tuple-element.551), channel_id=3, replica_groups=mesh['grp'=32,'harm'=16] {'harm'}, dimensions={0}, use_global_device_ids=true | all-gather | bytes 835584 | tf_op jit(solution)/shard_map/all_gather | solution.py:25
  147.4 18.4 %all-gather.2 = f32[256,768]{1,0:T(8,128)} all-gather(f32[16,768]{1,0:T(8,128)S(1)} %get-tuple-element.552), channel_id=4, replica_groups=mesh['grp'=32,'harm'=16] {'harm'}, dimensions={0}, use_global_device_ids=true | all-gather | bytes 835584 | tf_op jit(solution)/shard_map/all_gather | solution.py:25
  165.8 14.0 %while.97 = (s32[]{:T(128)}, f32[16,768]{1,0:T(8,128)S(1)}, f32[16,768]{1,0:T(8,128)S(1)}, f32[16,768]{1,0:T(8,128)S(1)}, s32[]{:T(128)}, /*index=5*/f32[16,16,7...) while((s32[]{:T(128)}, f32[16,768]{1,0:T(8,128)S(1)}, ...), condition=%wide.region_8.9_spmd.clone, body=%wide.region_7.8_spmd.clone.sunk | while | flops 159748 | bytes 442493 | solution.py:37
  179.8 8.0 %while.94 = (s32[]{:T(128)}, f32[16,768]{1,0:T(8,128)S(1)}, f32[8,768]{1,0:T(8,128)S(1)}, f32[8,768]{1,0:T(8,128)S(1)}, f32[16,768]{1,0:T(8,128)}, /*index=5*/f3...) while((s32[]{:T(128)}, f32[16,768]{1,0:T(8,128)S(1)}, f32[8,768]{1,0:T(8,128)S(1)}, ...), condition=%wide.region_11.12_spmd, body=%wide.region_9.11_spmd.sunk | while | flops 60674 | bytes 270437 | solution.py:74
  188.8 3.8 all-to-all-start.1
  192.7 4.7 copy.64
  199.2 2.5 scatter_custom_fusion.2
  208.5 110.2 %all-reduce.6.cloned.1.call-done = f32[64,512]{1,0:T(8,128)} async-done(((f32[64,512]{1,0:T(8,128)}), f32[64,512]{1,0:T(8,128)}) %all-reduce.6.cloned.1.call-update) | async-done | bytes 131088
  321.7 57.8 %reduce-scatter.5.cloned.1.call-done = f32[8,512]{1,0:T(8,128)} async-done(((f32[128,512]{1,0:T(8,128)}), f32[8,512]{1,0:T(8,128)}) %reduce-scatter.5.cloned.1.call-update) | async-done | bytes 16400 | tf_op jit(solution)/shard_map/reduce_scatter | solution.py:164
  380.3 2.8 scatter_custom_fusion.3
  383.4 17.5 %all_to_all.20 = f32[32,1,192]{2,1,0:T(1,128)S(1)} all-to-all(f32[32,1,192]{2,1,0:T(1,128)S(1)} %reshape.434), channel_id=1, replica_groups=mesh['grp'=32,'harm'=16] {'grp'}, dimensions={0} | all-to-all | bytes 49152 | tf_op jit(solution)/shard_map/all_to_all | solution.py:173
  401.9 2.9 collective-permute-start.5
  405.1 2.3 collective-permute-done.5
  408.1 20.3 %all-gather.3 = f32[256,768]{1,0:T(8,128)S(1)} all-gather(f32[16,768]{1,0:T(8,128)S(1)} %get-tuple-element.557), channel_id=5, replica_groups=mesh['grp'=32,'harm'=16] {'harm'}, dimensions={0}, use_global_device_ids=true | all-gather | bytes 835584 | tf_op jit(solution)/shard_map/all_gather | solution.py:25
  428.4 17.7 %all-gather.4 = f32[256,768]{1,0:T(8,128)S(1)} all-gather(f32[16,768]{1,0:T(8,128)S(1)} %get-tuple-element.558), channel_id=6, replica_groups=mesh['grp'=32,'harm'=16] {'harm'}, dimensions={0}, use_global_device_ids=true | all-gather | bytes 835584 | tf_op jit(solution)/shard_map/all_gather | solution.py:25
  446.1 18.2 %all-gather.5 = f32[256,768]{1,0:T(8,128)} all-gather(f32[16,768]{1,0:T(8,128)S(1)} %get-tuple-element.559), channel_id=7, replica_groups=mesh['grp'=32,'harm'=16] {'harm'}, dimensions={0}, use_global_device_ids=true | all-gather | bytes 835584 | tf_op jit(solution)/shard_map/all_gather | solution.py:25
  464.3 14.0 %while.99 = (s32[]{:T(128)}, f32[16,768]{1,0:T(8,128)S(1)}, f32[16,768]{1,0:T(8,128)S(1)}, f32[16,768]{1,0:T(8,128)S(1)}, s32[]{:T(128)}, /*index=5*/f32[16,16,7...) while((s32[]{:T(128)}, f32[16,768]{1,0:T(8,128)S(1)}, ...), condition=%wide.region_20.21_spmd.clone, body=%wide.region_19.20_spmd.clone.sunk | while | flops 159748 | bytes 442493 | solution.py:37
  480.8 3.9 all-to-all-start.3
  484.7 3.0 collective-permute-start.3
  489.0 4.3 all-to-all-done.3
  498.0 108.8 %all-reduce.8.cloned.1.call-done = f32[64,512]{1,0:T(8,128)} async-done(((f32[64,512]{1,0:T(8,128)}), f32[64,512]{1,0:T(8,128)}) %all-reduce.8.cloned.1.call-update) | async-done | bytes 131088
  606.8 2.3 multiply_subtract_fusion.1
  (261 shorter events, 81.0 us)
Async XLA Ops:
  7.2 185.5 %slice-start = ((f32[4,3,128,128]{3,2,1,0:T(8,128)}), f32[4,1,128,128]{3,2,1,0:T(8,128)S(1)}, s32[]{:S(2)}) async-start(f32[4,3,128,128]{3,2,1,0:T(8,128)} %param.24), calls=%async_computation.10 | async-start | bytes 524288 | tf_op jit(solution)/shard_map/slice | solution.py:133
  7.2 65.7 %reduce-scatter.3.cloned.1.call-start = ((), (), s32[]{:S(2)}) async-start(), calls=%async_computation.6 | async-start | bytes 278528 | tf_op jit(solution)/shard_map/reduce_scatter | solution.py:164
  10.0 197.9 %collective-permute-start = (f32[4,256]{1,0:T(4,128)S(1)}, f32[4,256]{1,0:T(4,128)S(1)}, u32[]{:S(2)}, u32[]{:S(2)}) collective-permute-start(f32[4,256]{1,0:T(4,128)S(1)} %get-tuple-element.824), channel_id=1, source_target_pairs={{0,16},{16,32},{32,48},{48,64},{64,80},{80,96},{96,112},{112,128},... | collective-permute-start | bytes 12296 | tf_op jit(solution)/shard_map/ppermute | solution.py:45
  14.8 193.1 %collective-permute-start.1 = (f32[4,256]{1,0:T(4,128)S(1)}, f32[4,256]{1,0:T(4,128)S(1)}, u32[]{:S(2)}, u32[]{:S(2)}) collective-permute-start(f32[4,256]{1,0:T(4,128)S(1)} %get-tuple-element.825), channel_id=1, source_target_pairs={{16,0},{32,16},{48,32},{64,48},{80,64},{96,80},{112,96},{128,112},... | collective-permute-start | bytes 12296 | tf_op jit(solution)/shard_map/ppermute | solution.py:48
  77.4 17.7 %all-to-all-start = ((f32[32,1,192]{2,1,0:T(1,128)}), f32[32,1,192]{2,1,0:T(1,128)S(1)}, u32[]{:S(2)}, u32[]{:S(2)}) async-start(f32[32,1,192]{2,1,0:T(1,128)} %reshape.430), calls=%async_computation.1 | async-start | bytes 65536 | tf_op jit(solution)/shard_map/all_to_all | solution.py:173
  96.6 5.4 collective-permute-start.2
  147.4 60.5 %copy-start.3 = (f32[4,512]{1,0:T(4,128)S(1)}, f32[4,512]{1,0:T(4,128)}, u32[]{:S(2)}) copy-start(f32[4,512]{1,0:T(4,128)} %param.21) | copy-start | bytes 24580
  147.4 171.3 %copy-start.2 = (f32[4,3,128,128]{3,2,1,0:T(8,128)S(1)}, f32[4,3,128,128]{3,2,1,0:T(8,128)}, u32[]{:S(2)}) copy-start(f32[4,3,128,128]{3,2,1,0:T(8,128)} %param.24) | copy-start | bytes 2359300
  147.4 171.3 %copy-start.4 = (f32[4,512]{1,0:T(4,128)S(1)}, f32[4,512]{1,0:T(4,128)}, u32[]{:S(2)}) copy-start(f32[4,512]{1,0:T(4,128)} %param.22) | copy-start | bytes 24580
  147.4 171.3 %copy-start.5 = (f32[512]{0:T(512)S(1)}, f32[512]{0:T(512)}, u32[]{:S(2)}) copy-start(f32[512]{0:T(512)} %param.23) | copy-start | bytes 6148
  187.8 219.5 %copy-start = (f32[16,768]{1,0:T(8,128)S(1)}, f32[16,768]{1,0:T(8,128)}, u32[]{:S(2)}) copy-start(f32[16,768]{1,0:T(8,128)} %get-tuple-element.1325) | copy-start | bytes 147460
  187.9 219.5 %copy-start.1 = (f32[16,768]{1,0:T(8,128)S(1)}, f32[16,768]{1,0:T(8,128)}, u32[]{:S(2)}) copy-start(f32[16,768]{1,0:T(8,128)} %get-tuple-element.1331) | copy-start | bytes 147460
  188.8 14.8 %all-to-all-start.1 = ((f32[32,1,192]{2,1,0:T(1,128)}), f32[32,1,192]{2,1,0:T(1,128)S(1)}, u32[]{:S(2)}, u32[]{:S(2)}) async-start(f32[32,1,192]{2,1,0:T(1,128)} %reshape.432), calls=%async_computation.2 | async-start | bytes 65536 | tf_op jit(solution)/shard_map/all_to_all | solution.py:181
  192.6 126.1 %all-reduce.6.cloned.1.call-start = ((), (), s32[]{:S(2)}) async-start(), calls=%async_computation.8 | async-start | bytes 262144
  207.7 171.8 %reduce-scatter.5.cloned.1.call-start = ((), (), s32[]{:S(2)}) async-start(), calls=%async_computation.7 | async-start | bytes 278528 | tf_op jit(solution)/shard_map/reduce_scatter | solution.py:164
  401.9 5.4 collective-permute-start.5
  480.8 12.6 %all-to-all-start.3 = ((f32[32,1,192]{2,1,0:T(1,128)}), f32[32,1,192]{2,1,0:T(1,128)S(1)}, u32[]{:S(2)}, u32[]{:S(2)}) async-start(f32[32,1,192]{2,1,0:T(1,128)} %reshape.436), calls=%async_computation.5 | async-start | bytes 65536 | tf_op jit(solution)/shard_map/all_to_all | solution.py:181
  484.6 122.2 %all-reduce.8.cloned.1.call-start = ((), (), s32[]{:S(2)}) async-start(), calls=%async_computation.9 | async-start | bytes 262144
  484.7 12.7 %collective-permute-start.3 = (f32[4,256]{1,0:T(4,128)S(1)}, f32[4,256]{1,0:T(4,128)S(1)}, u32[]{:S(2)}, u32[]{:S(2)}) collective-permute-start(f32[4,256]{1,0:T(4,128)S(1)} %get-tuple-element.822), channel_id=1, source_target_pairs={{0,16},{16,32},{32,48},{48,64},{64,80},{80,96},{96,112},{112,128},... | collective-permute-start | bytes 12296 | tf_op jit(solution)/shard_map/ppermute | solution.py:45
  487.7 9.7 %collective-permute-start.4 = (f32[4,256]{1,0:T(4,128)S(1)}, f32[4,256]{1,0:T(4,128)S(1)}, u32[]{:S(2)}, u32[]{:S(2)}) collective-permute-start(f32[4,256]{1,0:T(4,128)S(1)} %get-tuple-element.823), channel_id=1, source_target_pairs={{16,0},{32,16},{48,32},{64,48},{80,64},{96,80},{112,96},{128,112},... | collective-permute-start | bytes 12296 | tf_op jit(solution)/shard_map/ppermute | solution.py:48
Sparse Core Ops, SparseCore 0:
  10.8 62.0 reduce-scatter.2
  207.8 110.8 all-reduce.5
  321.8 57.6 reduce-scatter.4
  497.5 109.2 all-reduce.7
where the time goes:
time: 619 us; the launch traced here: 616 us
  waiting for transfers between devices  343 us (55%)
  blocking collectives  130 us (21%)
  other arithmetic  56 us (9%)
  starting transfers between devices  33.1 us (5%)
  local copies, waits for them, and re-layouts  27.4 us (4%)
  between operations  15.1 us (2%)
  matrix products  9.82 us (2%)
    unnamed x6, waiting for transfers between devices  219 us
    all_gather x6, blocking collectives, entering(): everything = jax.tree.map(lambda part: lax.all_gather(part, axis), array)  113 us
    reduce_scatter x2, waiting for transfers between devices, local(): lax.psum_scatter(jnp.dot(fourier_basis(rows, my_coefs, HARM, samples), co...  106 us
    select_n x32, other arithmetic, turn(): return jax.tree.map(lambda a, b: jnp.where(reached, a, b), new, before)  27.3 us
    all_to_all x1, blocking collectives, local(): lax.all_to_all(outgoing.reshape(row_count, groups, capacity), 'grp', spli...  17.5 us
  transfers between devices with their start and end apart: 13, of which 8 were waited for; matrix products, arithmetic and copies ran while one was open for 11% of the time, Pallas kernels for 0%

commit v1 on v0

v1 whole, which is shorter than its diff:
```python
import math

import jax
import jax.numpy as jnp
import numpy as np
from jax import lax
from jax.experimental import pallas as pl
from jax.experimental.pallas import tpu as pltpu
from jax.sharding import PartitionSpec as P

HARM = 32
NT = 128
GRP = 32
PARTS = 16
CHIPS = 8
CD = 4
DOF = 512
JOINTS = 256
CAP = 24
NE = 16
f32, bf16, i32 = jnp.float32, jnp.bfloat16, jnp.int32
MESH = pl.DeviceIdType.MESH


def basis_tables():
    row = np.arange(PARTS * 8)
    coef = 4 * (row // 8) + row % 4
    harmonic = np.where(coef <= HARM, coef, coef - HARM)
    angle = 2.0 * math.pi * ((np.arange(NT)[:, None] * harmonic[None, :]) % NT) / NT
    synth = np.where(coef > HARM, np.sin(angle), np.cos(angle))
    move = (synth - np.roll(synth, 1, axis=0)) * np.where(row % 8 < 4, 1.0, -1.0)
    project = (synth * np.where(coef == 0, 1.0, 2.0) / NT).T

    def split(x):
        x = x.astype(np.float32)
        high = x.astype(jnp.bfloat16)
        return [high, (x - high.astype(np.float32)).astype(jnp.bfloat16)]

    return np.stack(split(move) + split(project))


def split2(x):
    high = x.astype(bf16).astype(f32)
    return high, x - high


def terms2(x):
    return jnp.concatenate(split2(x), axis=0).astype(bf16)


def terms3(x):
    high, rest = split2(x)
    mid, low = split2(rest)
    return jnp.concatenate([high, mid, low], axis=0).astype(bf16)


def mm(a, b):
    return lax.dot_general(a, b, (((1,), (0,)), ((), ())), preferred_element_type=f32)


def mm_t(a, b):
    return lax.dot_general(a, b, (((1,), (1,)), ((), ())), preferred_element_type=f32)


def select3(x, weights, product):
    n = x.shape[0]
    y = product(terms3(x), weights)
    return y[:n] + y[n : 2 * n] + y[2 * n :]


def kernel(
    u_hbm,
    load_hbm,
    mass_hbm,
    offset_hbm,
    dofs_hbm,
    owner_hbm,
    basis_hbm,
    stiff_hbm,
    k_hbm,
    s_hbm,
    out_u,
    out_r,
    u_v,
    load_v,
    mass_v,
    offset_v,
    dofs_v,
    owner_v,
    basis_v,
    stiff_v,
    table_v,
    near_hi,
    near_lo,
    far_hi,
    far_lo,
    perm,
    slots,
    send1,
    recv1,
    send2,
    recv2,
    sendp,
    recvp,
    move_v,
    total_v,
    sendg,
    recvg,
    current,
    halo,
    local_sem,
    send_sem,
    recv_sem,
    halo_send,
    halo_recv,
):
    g = lax.axis_index("grp")
    h = lax.axis_index("harm")
    chip = lax.div(h, 2)
    core = lax.rem(h, 2)
    right = lax.rem(g + 1, GRP)
    left = lax.rem(g + GRP - 1, GRP)

    fetches = [
        pltpu.make_async_copy(src, dst, local_sem.at[i])
        for i, (src, dst) in enumerate(
            [
                (owner_hbm, owner_v),
                (dofs_hbm, dofs_v),
                (u_hbm, u_v),
                (load_hbm, load_v),
                (mass_hbm, mass_v),
                (offset_hbm, offset_v),
                (k_hbm, table_v.at[0]),
                (s_hbm, table_v.at[1]),
                (stiff_hbm, stiff_v),
                (basis_hbm, basis_v),
            ]
        )
    ]
    for fetch in fetches:
        fetch.start()

    barrier = pltpu.get_barrier_semaphore()
    for k in range(1, PARTS):
        pl.semaphore_signal(
            barrier, inc=1, device_id=(g, lax.rem(h + k, PARTS)), device_id_type=MESH
        )
    for side in (left, right):
        pl.semaphore_signal(barrier, inc=1, device_id=(side, h), device_id_type=MESH)
    source_part = lax.rem(lax.div(g, 2) + PARTS - 2, PARTS)
    for k in range(4):
        pl.semaphore_signal(
            barrier, inc=1, device_id=(4 * chip + k, source_part), device_id_type=MESH
        )

    fetches[0].wait()
    fetches[1].wait()
    owner = owner_v[...]
    own = jnp.where(lax.broadcasted_iota(i32, (GRP, JOINTS), 0) == owner, 1.0, 0.0)
    before = jnp.where(
        lax.broadcasted_iota(i32, (JOINTS, JOINTS), 0)
        < lax.broadcasted_iota(i32, (JOINTS, JOINTS), 1),
        1.0,
        0.0,
    )
    earlier = mm(own.astype(bf16), before.astype(bf16))
    rank = jnp.sum(earlier * own, axis=0, keepdims=True).astype(i32)
    slot = (owner >> 2) * 128 + (owner & 3) * CAP + rank
    row = lax.broadcasted_iota(i32, (128, JOINTS), 0)
    for m in range(CHIPS):
        slots[m * 128 : (m + 1) * 128, :] = jnp.where(row == slot - m * 128, 1.0, 0.0).astype(bf16)
    dofs = dofs_v[...]
    row = lax.broadcasted_iota(i32, (128, DOF), 0)
    for m in range(DOF // 128):
        perm[m * 128 : (m + 1) * 128, :] = jnp.where(row == dofs - m * 128, 1.0, 0.0).astype(bf16)

    fetches[6].wait()
    fetches[7].wait()
    target = 2 * lax.rem(h + 2, PARTS)
    lane = lax.broadcasted_iota(i32, (NE, 128), 1)
    first = lax.rem(g, 4) * CAP
    wanted = (lane >= first) & (lane < first + CAP)
    for t in range(2):
        column = (target + t) * CAP
        tile = jnp.minimum(lax.div(column, 128), 4)
        shift = lax.rem(first - (column - tile * 128) + 512, 256)
        for a in range(2):
            part = table_v[a, 0, :, pl.ds(pl.multiple_of(tile * 128, 128), 256)]
            rolled = pltpu.roll(part, shift, 1)[:, :128]
            sendp[t, a * NE : (a + 1) * NE, :] = jnp.where(wanted, rolled, 0.0)

    fetches[8].wait()
    eye = lax.broadcasted_iota(i32, (128, 128), 0) == lax.broadcasted_iota(i32, (128, 128), 1)
    diagonals = []

    def store(hi, lo, i, at, block):
        high, low = split2(block)
        hi[i, :, at : at + 128] = high.astype(bf16)
        lo[i, :, at : at + 128] = low.astype(bf16)

    for i in range(4):
        own_block = stiff_v[i, 0]
        diagonals.append(jnp.sum(jnp.where(eye, own_block, 0.0), axis=0, keepdims=True))
        store(near_hi, near_lo, i, 0, jnp.where(eye, 0.0, own_block))
        store(near_hi, near_lo, i, 128, stiff_v[i, 2 if i < 2 else 1])
        store(far_hi, far_lo, i, 0, stiff_v[i, 1 if i < 2 else 2])
    kdiag = jnp.concatenate(diagonals, axis=1)
    coef = 4 * h + lax.broadcasted_iota(i32, (CD, DOF), 0)
    freq = jnp.where(coef <= HARM, coef, coef - HARM).astype(f32) * (1.0 / HARM)
    fetches[4].wait()
    net = kdiag - (freq * freq) * mass_v[...]
    precond = 1.0 / net

    fetches[2].wait()
    u0 = u_v[...]
    upper = lax.broadcasted_iota(i32, (8, 128), 0) < CD

    def to_slots(x, sign, out):
        pairs = select3(x, perm[...], mm)
        relative = pairs[:, :JOINTS] + sign * pairs[:, JOINTS:]
        by_slot = select3(relative, slots[...], mm_t)
        for m in range(CHIPS):
            out[m] = by_slot[:, m * 128 : (m + 1) * 128]

    sign = jnp.where(lax.broadcasted_iota(i32, (8, JOINTS), 0) < CD, -1.0, 1.0)
    to_slots(jnp.concatenate([u0, precond], axis=0), sign, send1)

    pl.semaphore_wait(barrier, PARTS - 1 + 2 + 4)

    def send_halo(n, ref):
        copies = [
            pltpu.make_async_remote_copy(
                src_ref=ref.at[:, 256:512] if k == 0 else ref.at[:, 0:256],
                dst_ref=halo.at[n, k],
                send_sem=halo_send.at[n, k],
                recv_sem=halo_recv.at[n, k],
                device_id=(side, h),
                device_id_type=MESH,
            )
            for k, side in enumerate((right, left))
        ]
        for copy in copies:
            copy.start()
        return copies

    halo0 = send_halo(0, u_v)

    def send_parts(n, src, dst):
        for k in range(1, PARTS):
            to = lax.rem(h + k, PARTS)
            pltpu.make_async_remote_copy(
                src_ref=src.at[lax.div(to, 2)],
                dst_ref=dst.at[h],
                send_sem=send_sem.at[n],
                recv_sem=recv_sem.at[n],
                device_id=(g, to),
                device_id_type=MESH,
            ).start()
        dst[h] = src[chip]

    def settle(ref, sem):
        pltpu.make_async_copy(ref, ref, sem).wait()

    send_parts(0, send1, recv1)
    for t in range(2):
        for c in range(2):
            pltpu.make_async_remote_copy(
                src_ref=sendp.at[t],
                dst_ref=recvp.at[lax.rem(g, 4)],
                send_sem=send_sem.at[2],
                recv_sem=recv_sem.at[2],
                device_id=(target + t, 2 * lax.div(g, 4) + c),
                device_id_type=MESH,
            ).start()

    fetches[5].wait()
    offset = offset_v[...]

    def block(u, i):
        return u[:, i * 128 : (i + 1) * 128]

    def nearer(i, k):
        return jnp.abs(offset[i : i + 1, k : k + 1]) == 1

    def apply(lhs, hi, lo):
        terms = terms2(lhs)
        a = mm_t(terms, hi)
        b = mm_t(terms, lo)
        return a[:CD] + (a[CD:] + b[:CD])

    def near_product(u):
        parts = []
        for i in range(4):
            if i < 2:
                other = jnp.where(nearer(i, 1), block(u, i + 1), block(u, i + 2))
            else:
                other = jnp.where(nearer(i, 0), block(u, i - 1), block(u, i - 2))
            lhs = jnp.concatenate([block(u, i), other], axis=1)
            parts.append(apply(lhs, near_hi[i], near_lo[i]))
        return jnp.concatenate(parts, axis=1)

    def far_product(u, n):
        low = jnp.where(g > 0, halo[n, 0], 0.0)
        high = jnp.where(g < GRP - 1, halo[n, 1], 0.0)
        others = [
            jnp.where(nearer(0, 0), block(low, 1), block(low, 0)),
            jnp.where(nearer(1, 0), block(u, 0), block(low, 1)),
            jnp.where(nearer(2, 1), block(u, 3), block(high, 0)),
            jnp.where(nearer(3, 1), block(high, 0), block(high, 1)),
        ]
        return jnp.concatenate(
            [apply(others[i], far_hi[i], far_lo[i]) for i in range(4)], axis=1
        )

    fetches[3].wait()
    load = load_v[...]
    part = load - near_product(u0)
    for copy in halo0:
        copy.wait_recv()
    base = precond * (part - far_product(u0, 0))
    to_slots(jnp.concatenate([base, jnp.zeros_like(base)], axis=0), -1.0, send2)
    send_parts(1, send2, recv2)

    fetches[9].wait()
    settle(recv1.at[pl.ds(0, PARTS - 1)], recv_sem.at[0])
    settle(recvp, recv_sem.at[2])
    table = recvp[0] + recvp[1] + recvp[2] + recvp[3]
    k_slot = table[:NE]
    s_slot = table[NE:]

    def forces(x, n):
        high, low = split2(x)
        high, low = high.astype(bf16), low.astype(bf16)
        move_v[...] = mm(basis_v[0], high) + (mm(basis_v[1], high) + mm(basis_v[0], low))

        def samples(i, force):
            at = pl.multiple_of(8 * i, 8)
            move = move_v[pl.ds(at, 8), :]
            sums = []
            for j in range(8):
                force = jnp.clip(force + k_slot * move[j : j + 1, :], -s_slot, s_slot)
                sums.append(jnp.sum(force, axis=0, keepdims=True))
            total_v[pl.ds(at, 8), :] = jnp.concatenate(sums, axis=0)
            return force

        lax.fori_loop(0, NT // 8, samples, jnp.zeros((NE, 128), f32))
        high, low = split2(total_v[...])
        high, low = high.astype(bf16), low.astype(bf16)
        coefs = mm(basis_v[2], high) + (mm(basis_v[3], high) + mm(basis_v[2], low))
        sendg[n] = coefs.reshape(PARTS, 8, 128)
        for k in range(1, CHIPS):
            to = lax.rem(chip + k, CHIPS) * 2 + core
            pltpu.make_async_remote_copy(
                src_ref=sendg.at[n, to],
                dst_ref=recvg.at[n, chip],
                send_sem=send_sem.at[3 + n],
                recv_sem=recv_sem.at[3 + n],
                device_id=(g, to),
                device_id_type=MESH,
            ).start()
        recvg[n, chip] = sendg[n, h]

    def nonlinear(n):
        settle(recvg.at[n, pl.ds(0, CHIPS - 1)], recv_sem.at[3 + n])
        lanes = jnp.concatenate([recvg[n, m][:CD] for m in range(CHIPS)], axis=1)
        joint = select3(lanes, slots[...], mm)
        return select3(jnp.concatenate([joint, -joint], axis=1), perm[...], mm_t)

    first_part = upper[None]
    forces(jnp.where(first_part, recv1[...], 0.0).reshape(PARTS * 8, 128), 0)
    settle(recv2.at[pl.ds(0, PARTS - 1)], recv_sem.at[1])
    forces(jnp.where(first_part, recv2[...], recv1[...] * sendg[0]).reshape(PARTS * 8, 128), 1)

    u1 = base - precond * nonlinear(0)
    current[...] = u1
    halo1 = send_halo(1, current)
    part = near_product(u1) + net * u1 - load
    for copy in halo1:
        copy.wait_recv()
    part = part + far_product(u1, 1)
    residual = part + nonlinear(1)
    out_r[...] = residual
    out_u[...] = u1 - precond * residual

    for copy in halo0 + halo1:
        copy.wait_send()
    settle(recv1.at[pl.ds(0, PARTS - 1)], send_sem.at[0])
    settle(recv2.at[pl.ds(0, PARTS - 1)], send_sem.at[1])
    settle(recvp, send_sem.at[2])
    for n in range(2):
        settle(recvg.at[n, pl.ds(0, CHIPS - 1)], send_sem.at[3 + n])


def local(u, load, mass, stiffness, offset, dofs, owner, k_table, s_table):
    basis = jnp.asarray(basis_tables())
    hbm = pl.BlockSpec(memory_space=pltpu.HBM)
    vmem = pl.BlockSpec(memory_space=pltpu.VMEM)
    return pl.pallas_call(
        kernel,
        out_shape=[jax.ShapeDtypeStruct((CD, DOF), f32)] * 2,
        in_specs=[hbm] * 10,
        out_specs=[vmem] * 2,
        scratch_shapes=[
            pltpu.VMEM((CD, DOF), f32),
            pltpu.VMEM((CD, DOF), f32),
            pltpu.VMEM((1, DOF), f32),
            pltpu.VMEM((4, 2), i32),
            pltpu.VMEM((1, DOF), i32),
            pltpu.VMEM((1, JOINTS), i32),
            pltpu.VMEM((4, 128, 128), bf16),
            pltpu.VMEM((4, 3, 128, 128), f32),
            pltpu.VMEM((2, 1, NE, GRP * CAP), f32),
            pltpu.VMEM((4, 128, 256), bf16),
            pltpu.VMEM((4, 128, 256), bf16),
            pltpu.VMEM((4, 128, 128), bf16),
            pltpu.VMEM((4, 128, 128), bf16),
            pltpu.VMEM((DOF, DOF), bf16),
            pltpu.VMEM((CHIPS * 128, JOINTS), bf16),
            pltpu.VMEM((CHIPS, 8, 128), f32),
            pltpu.VMEM((PARTS, 8, 128), f32),
            pltpu.VMEM((CHIPS, 8, 128), f32),
            pltpu.VMEM((PARTS, 8, 128), f32),
            pltpu.VMEM((2, 2 * NE, 128), f32),
            pltpu.VMEM((4, 2 * NE, 128), f32),
            pltpu.VMEM((NT, 128), f32),
            pltpu.VMEM((NT, 128), f32),
            pltpu.VMEM((2, PARTS, 8, 128), f32),
            pltpu.VMEM((2, CHIPS, 8, 128), f32),
            pltpu.VMEM((CD, DOF), f32),
            pltpu.VMEM((2, 2, CD, 256), f32),
            pltpu.SemaphoreType.DMA((10,)),
            pltpu.SemaphoreType.DMA((5,)),
            pltpu.SemaphoreType.DMA((5,)),
            pltpu.SemaphoreType.DMA((2, 2)),
            pltpu.SemaphoreType.DMA((2, 2)),
        ],
        compiler_params=pltpu.CompilerParams(
            collective_id=0, has_side_effects=True, vmem_limit_bytes=16 * 2**20
        ),
    )(u, load, mass.reshape(1, DOF), offset, dofs, owner, basis, stiffness, k_table, s_table)


def solution(mesh):
    in_specs = (
        P("harm", "grp"),
        P("harm", "grp"),
        P("grp"),
        P("grp", None, None, None),
        P("grp", None),
        P("grp", None),
        P("grp", None),
        P("grp", None, None),
        P("grp", None, None),
    )
    out_specs = (P("harm", "grp"), P("harm", "grp"))

    def run(*args):
        return tuple(local(*args))

    return jax.shard_map(run, mesh=mesh, in_specs=in_specs, out_specs=out_specs, check_vma=False)
```

time: 619 us -> 48.9 us (0.08)
  the two profiles are of different devices: /device:TPU:1 before, /device:TPU:2 now
where the time goes in v1:
time: 48.9 us; the launch traced here: 48.5 us
  Pallas kernels  40.1 us (82%)
  local copies, waits for them, and re-layouts  7.69 us (16%)
  between operations  0.66 us (1%)
    pallas_call x1, Pallas kernels, local(): pl.pallas_call(kernel, out_shape=[jax.ShapeDtypeStruct((CD, DOF), f32)] *...  40.1 us
    unnamed x21, local copies, waits for them, and re-layouts  7.69 us

profile of v1, /device:TPU:2, one launch (start us, length us, event | category | flops | bytes accessed | tf_op | source)
XLA Modules:
  0.0 48.5 jit_solution(1521472652765619450)
XLA Ops:
  0.6 0.0 copy-start.7
  0.6 0.0 copy-start.6
  0.7 0.8 %copy.12.offset_hbm = s32[4,2]{1,0:T(4,128)S(1)} copy(s32[4,2]{0,1:T(2,128)} %param.14) | data formatting | bytes 64 | tf_op args[4]
  1.4 0.0 copy-done.7
  1.4 0.0 copy-done.6
  1.4 0.0 copy-start
  1.4 1.1 %copy-done = f32[4,3,128,128]{3,2,1,0:T(8,128)S(1)} copy-done((f32[4,3,128,128]{3,2,1,0:T(8,128)S(1)}, f32[4,3,128,128]{3,2,1,0:T(8,128)}, u32[]{:S(2)}) %copy-start) | copy-done | bytes 786456
  2.6 0.0 copy-start.1
  2.6 0.9 %copy-done.1 = bf16[4,128,128]{2,1,0:T(8,128)(2,1)S(1)} copy-done((bf16[4,128,128]{2,1,0:T(8,128)(2,1)S(1)}, bf16[4,128,128]{2,1,0:T(8,128)(2,1)}, u32[]{:S(2)}) %copy-start.1) | copy-done | bytes 131096
  3.5 0.0 copy-start.2
  3.5 0.8 %copy-done.2 = f32[1,16,768]{2,1,0:T(8,128)S(1)} copy-done((f32[1,16,768]{2,1,0:T(8,128)S(1)}, f32[1,16,768]{2,1,0:T(8,128)}, u32[]{:S(2)}) %copy-start.2) | copy-done | bytes 49176
  4.3 0.0 copy-start.3
  4.3 0.8 %copy-done.3 = f32[1,16,768]{2,1,0:T(8,128)S(1)} copy-done((f32[1,16,768]{2,1,0:T(8,128)S(1)}, f32[1,16,768]{2,1,0:T(8,128)}, u32[]{:S(2)}) %copy-start.3) | copy-done | bytes 49176
  5.1 0.0 copy-start.4
  5.1 0.7 %copy-done.4 = f32[4,512]{1,0:T(4,128)S(1)} copy-done((f32[4,512]{1,0:T(4,128)S(1)}, f32[4,512]{1,0:T(4,128)}, u32[]{:S(2)}) %copy-start.4) | copy-done | bytes 8216
  5.8 0.0 copy-start.5
  5.8 0.7 %copy-done.5 = f32[4,512]{1,0:T(4,128)S(1)} copy-done((f32[4,512]{1,0:T(4,128)S(1)}, f32[4,512]{1,0:T(4,128)}, u32[]{:S(2)}) %copy-start.5) | copy-done | bytes 8216
  6.5 0.0 copy-start.8
  6.5 0.7 %copy-done.8 = s32[1,256]{1,0:T(1,128)S(1)} copy-done((s32[1,256]{1,0:T(1,128)S(1)}, s32[1,256]{1,0:T(1,128)}, u32[]{:S(2)}) %copy-start.8) | copy-done | bytes 1048
  7.1 40.1 %shard_map.113 = (f32[4,512]{1,0:T(4,128)S(1)}, f32[4,512]{1,0:T(4,128)S(1)}) custom-call(f32[4,512]{1,0:T(4,128)S(1)} %copy-done.4, f32[4,512]{1,0:T(4,128)S(1)} %copy-done.5, f32[1,512]{1,0:T(1,128)S(1)} %bitcast.1, s32[4,2]{1,0:T(4,128)S(1)} %copy.12.offset_hbm, s32[1,512]{1,0:T(1,128)S(1)} %copy-done.7, s32[1,256]{1,0:T(1,128)S(1)} %copy-done.8, ...), custom_call_target="tpu_custom_call" | custom-call | tf_op jit(solution)/shard_map/pallas_call | solution.py:399
  47.3 0.6 %copy.15 = f32[4,512]{1,0:T(4,128)} copy(f32[4,512]{1,0:T(4,128)S(1)} %get-tuple-element.4) | data formatting | bytes 16384
  47.9 0.6 %copy.16 = f32[4,512]{1,0:T(4,128)} copy(f32[4,512]{1,0:T(4,128)S(1)} %get-tuple-element.5) | data formatting | bytes 16384
Async XLA Ops:
  0.6 0.8 %copy-start.7 = (s32[1,512]{1,0:T(1,128)S(1)}, s32[1,512]{1,0:T(1,128)}, u32[]{:S(2)}) copy-start(s32[1,512]{1,0:T(1,128)} %dofs_hbm.1) | copy-start | bytes 6148
  0.6 0.8 %copy-start.6 = (f32[512]{0:T(512)S(1)}, f32[512]{0:T(512)}, u32[]{:S(2)}) copy-start(f32[512]{0:T(512)} %param.12) | copy-start | bytes 6148
  1.4 1.1 %copy-start = (f32[4,3,128,128]{3,2,1,0:T(8,128)S(1)}, f32[4,3,128,128]{3,2,1,0:T(8,128)}, u32[]{:S(2)}) copy-start(f32[4,3,128,128]{3,2,1,0:T(8,128)} %stiff_hbm.1) | copy-start | bytes 2359300
  2.6 0.9 %copy-start.1 = (bf16[4,128,128]{2,1,0:T(8,128)(2,1)S(1)}, bf16[4,128,128]{2,1,0:T(8,128)(2,1)}, u32[]{:S(2)}) copy-start(bf16[4,128,128]{2,1,0:T(8,128)(2,1)} %constant.2.clone.basis_hbm) | copy-start | bytes 393220
  3.5 0.8 %copy-start.2 = (f32[1,16,768]{2,1,0:T(8,128)S(1)}, f32[1,16,768]{2,1,0:T(8,128)}, u32[]{:S(2)}) copy-start(f32[1,16,768]{2,1,0:T(8,128)} %k_hbm.1) | copy-start | bytes 147460
  4.3 0.8 %copy-start.3 = (f32[1,16,768]{2,1,0:T(8,128)S(1)}, f32[1,16,768]{2,1,0:T(8,128)}, u32[]{:S(2)}) copy-start(f32[1,16,768]{2,1,0:T(8,128)} %s_hbm.1) | copy-start | bytes 147460
  5.1 0.7 %copy-start.4 = (f32[4,512]{1,0:T(4,128)S(1)}, f32[4,512]{1,0:T(4,128)}, u32[]{:S(2)}) copy-start(f32[4,512]{1,0:T(4,128)} %u_hbm.1) | copy-start | bytes 24580
  5.8 0.7 %copy-start.5 = (f32[4,512]{1,0:T(4,128)S(1)}, f32[4,512]{1,0:T(4,128)}, u32[]{:S(2)}) copy-start(f32[4,512]{1,0:T(4,128)} %load_hbm.1) | copy-start | bytes 24580
  6.5 0.7 %copy-start.8 = (s32[1,256]{1,0:T(1,128)S(1)}, s32[1,256]{1,0:T(1,128)}, u32[]{:S(2)}) copy-start(s32[1,256]{1,0:T(1,128)} %owner_hbm.1) | copy-start | bytes 3076

commit v2 on v1

v2 whole, which is shorter than its diff:
```python
import math

import jax
import jax.numpy as jnp
import numpy as np
from jax import lax
from jax.experimental import pallas as pl
from jax.experimental.pallas import tpu as pltpu
from jax.sharding import PartitionSpec as P

HARM = 32
NT = 128
GRP = 32
PARTS = 16
CHIPS = 8
CD = 4
DOF = 512
JOINTS = 256
CAP = 24
NE = 16
f32, bf16, i32 = jnp.float32, jnp.bfloat16, jnp.int32
MESH = pl.DeviceIdType.MESH


def basis_tables():
    row = np.arange(PARTS * 8)
    coef = 4 * (row // 8) + row % 4
    harmonic = np.where(coef <= HARM, coef, coef - HARM)
    angle = 2.0 * math.pi * ((np.arange(NT)[:, None] * harmonic[None, :]) % NT) / NT
    synth = np.where(coef > HARM, np.sin(angle), np.cos(angle))
    move = (synth - np.roll(synth, 1, axis=0)) * np.where(row % 8 < 4, 1.0, -1.0)
    project = (synth * np.where(coef == 0, 1.0, 2.0) / NT).T

    def split(x):
        x = x.astype(np.float32)
        high = x.astype(jnp.bfloat16)
        return [high, (x - high.astype(np.float32)).astype(jnp.bfloat16)]

    short = np.zeros((NT, 128))
    short[:, : PARTS * CD] = move[:, row % 8 < 4]
    return np.stack(split(move) + split(project) + split(short))


def split2(x):
    high = x.astype(bf16).astype(f32)
    return high, x - high


def terms2(x):
    return jnp.concatenate(split2(x), axis=0).astype(bf16)


def terms3(x):
    high, rest = split2(x)
    mid, low = split2(rest)
    return jnp.concatenate([high, mid, low], axis=0).astype(bf16)


def mm(a, b):
    return lax.dot_general(a, b, (((1,), (0,)), ((), ())), preferred_element_type=f32)


def mm_t(a, b):
    return lax.dot_general(a, b, (((1,), (1,)), ((), ())), preferred_element_type=f32)


def select3(x, weights, product):
    n = x.shape[0]
    y = product(terms3(x), weights)
    return y[:n] + y[n : 2 * n] + y[2 * n :]


def kernel(
    u_hbm,
    load_hbm,
    mass_hbm,
    offset_hbm,
    dofs_hbm,
    owner_hbm,
    basis_hbm,
    stiff_hbm,
    k_hbm,
    s_hbm,
    out_u,
    out_r,
    u_v,
    load_v,
    mass_v,
    offset_v,
    dofs_v,
    owner_v,
    basis_v,
    stiff_v,
    table_v,
    near_hi,
    near_lo,
    far_hi,
    far_lo,
    perm,
    slots,
    slots_side,
    send1,
    recv1,
    send2,
    recv2,
    sendp,
    recvp,
    move_v,
    total_v,
    sendg,
    recvg,
    recvg_side,
    fixed,
    fixed_side,
    base_v,
    base_side,
    u_side,
    local_sem,
    send_sem,
    recv_sem,
    side_send,
    side_recv,
):
    g = lax.axis_index("grp")
    h = lax.axis_index("harm")
    chip = lax.div(h, 2)
    core = lax.rem(h, 2)
    sides = (lax.rem(g + 1, GRP), lax.rem(g + GRP - 1, GRP))

    barrier = pltpu.get_barrier_semaphore()

    def greet(group, part):
        pl.semaphore_signal(barrier, inc=1, device_id=(group, part), device_id_type=MESH)

    source = 4 * lax.rem(chip + GRP - g, CHIPS)
    for k in range(4):
        greet(source + k, 2 * chip + 1 - core)
    for k in (4, 3, 5, 2, 6, 1, 7, 0):
        part = 2 * lax.rem(chip + k, CHIPS)
        for side in sides:
            greet(side, part + core)
        if k > 0:
            greet(g, part + core)
        greet(g, part + 1 - core)

    fetches = [
        pltpu.make_async_copy(src, dst, local_sem.at[i])
        for i, (src, dst) in enumerate(
            [
                (owner_hbm, owner_v),
                (dofs_hbm, dofs_v),
                (u_hbm, u_v),
                (load_hbm, load_v),
                (mass_hbm, mass_v),
                (offset_hbm, offset_v),
                (k_hbm, table_v.at[0]),
                (s_hbm, table_v.at[1]),
                (stiff_hbm, stiff_v),
                (basis_hbm, basis_v),
            ]
        )
    ]
    for fetch in fetches:
        fetch.start()

    fetches[0].wait()
    fetches[1].wait()
    owner = owner_v[...]
    own = jnp.where(lax.broadcasted_iota(i32, (GRP, JOINTS), 0) == owner, 1.0, 0.0)
    before = jnp.where(
        lax.broadcasted_iota(i32, (JOINTS, JOINTS), 0)
        < lax.broadcasted_iota(i32, (JOINTS, JOINTS), 1),
        1.0,
        0.0,
    )
    earlier = mm(own.astype(bf16), before.astype(bf16))
    rank = jnp.sum(earlier * own, axis=0, keepdims=True)
    tile = (((owner >> 2) + g) & 7).astype(f32)
    lane = ((owner & 3) * CAP).astype(f32) + rank
    ones = jnp.ones((1, JOINTS), f32)
    dofs = dofs_v[...]
    row = lax.broadcasted_iota(i32, (128, DOF), 0)
    for m in range(DOF // 128):
        perm[m * 128 : (m + 1) * 128, :] = jnp.where(row == dofs - m * 128, 1.0, 0.0).astype(bf16)
    by_joint = jnp.concatenate(
        [
            jnp.concatenate([tile, lane, ones], axis=0),
            jnp.concatenate([tile, lane, -ones], axis=0),
        ],
        axis=1,
    )
    by_dof = mm_t(by_joint.astype(bf16), perm[...])
    slot_f = by_dof[0:1] * 128.0 + by_dof[1:2]
    slot = slot_f.astype(i32)
    sign = by_dof[2:3]
    for m in range(CHIPS):
        slots[m * 128 : (m + 1) * 128, :] = jnp.where(row == slot - m * 128, 1.0, 0.0).astype(bf16)

    fetches[2].wait()
    u0 = u_v[...]

    def to_slots(x, out):
        by_slot = select3(x, slots[...], mm_t)
        for m in range(CHIPS):
            out[m] = by_slot[:, m * 128 : (m + 1) * 128]

    to_slots(u0 * sign, send1)

    fetches[6].wait()
    fetches[7].wait()
    target = lax.rem(chip + CHIPS - lax.div(g, 4), CHIPS)
    at = lax.broadcasted_iota(i32, (NE, 128), 1)
    first = lax.rem(g, 4) * CAP
    wanted = (at >= first) & (at < first + CAP)
    for t in range(4):
        column = (target + 8 * t) * CAP
        begin = jnp.minimum(lax.div(column, 128), 4)
        shift = lax.rem(first - (column - begin * 128) + 512, 256)
        for a in range(2):
            part = table_v[a, 0, :, pl.ds(pl.multiple_of(begin * 128, 128), 256)]
            rolled = pltpu.roll(part, shift, 1)[:, :128]
            sendp[t, a * NE : (a + 1) * NE, :] = jnp.where(wanted, rolled, 0.0)

    pl.semaphore_wait(barrier, PARTS - 1 + 2 * CHIPS + 4)

    def send_sides(n, src, dst):
        copies = [
            pltpu.make_async_remote_copy(
                src_ref=src.at[:, 256:512] if k == 0 else src.at[:, 0:256],
                dst_ref=dst.at[k],
                send_sem=side_send.at[n, k],
                recv_sem=side_recv.at[n, k],
                device_id=(side, h),
                device_id_type=MESH,
            )
            for k, side in enumerate(sides)
        ]
        for copy in copies:
            copy.start()
        return copies

    def send_parts(n, src, dst):
        for k in (8, 7, 9, 6, 10, 5, 11, 4, 12, 3, 13, 2, 14, 1, 15):
            to = lax.rem(h + k, PARTS)
            pltpu.make_async_remote_copy(
                src_ref=src.at[lax.div(to, 2)],
                dst_ref=dst.at[h],
                send_sem=send_sem.at[n],
                recv_sem=recv_sem.at[n],
                device_id=(g, to),
                device_id_type=MESH,
            ).start()
        dst[h] = src[chip]

    def settle(ref, sem):
        pltpu.make_async_copy(ref, ref, sem).wait()

    halo0 = send_sides(0, u_v, u_side)
    for t in range(4):
        pltpu.make_async_remote_copy(
            src_ref=sendp.at[t],
            dst_ref=recvp.at[lax.rem(g, 4)],
            send_sem=send_sem.at[2],
            recv_sem=recv_sem.at[2],
            device_id=(target + 8 * t, 2 * chip + 1 - core),
            device_id_type=MESH,
        ).start()
    send_parts(0, send1, recv1)

    fetches[8].wait()
    eye = lax.broadcasted_iota(i32, (128, 128), 0) == lax.broadcasted_iota(i32, (128, 128), 1)
    diagonals = []

    def store(hi, lo, i, at, block):
        high, low = split2(block)
        hi[i, :, at : at + 128] = high.astype(bf16)
        lo[i, :, at : at + 128] = low.astype(bf16)

    for i in range(4):
        own_block = stiff_v[i, 0]
        diagonals.append(jnp.sum(jnp.where(eye, own_block, 0.0), axis=0, keepdims=True))
        store(near_hi, near_lo, i, 0, jnp.where(eye, 0.0, own_block))
        store(near_hi, near_lo, i, 128, stiff_v[i, 2 if i < 2 else 1])
        store(far_hi, far_lo, i, 0, stiff_v[i, 1 if i < 2 else 2])
    kdiag = jnp.concatenate(diagonals, axis=1)
    coef = 4 * h + lax.broadcasted_iota(i32, (CD, DOF), 0)
    freq = jnp.where(coef <= HARM, coef, coef - HARM).astype(f32) * (1.0 / HARM)
    fetches[4].wait()
    net = kdiag - (freq * freq) * mass_v[...]
    precond = 1.0 / net
    signed = precond * sign
    fixed[...] = jnp.concatenate([signed, jnp.broadcast_to(slot_f, (CD, DOF))], axis=0)
    halof = send_sides(1, fixed, fixed_side)

    fetches[5].wait()
    offset = offset_v[...]

    def block(u, i):
        return u[:, i * 128 : (i + 1) * 128]

    def nearer(i, k):
        return jnp.abs(offset[k : k + 1, i : i + 1]) == 1

    def apply(lhs, hi, lo):
        terms = terms2(lhs)
        a = mm_t(terms, hi)
        b = mm_t(terms, lo)
        return a[:CD] + (a[CD:] + b[:CD])

    def near_product(u):
        parts = []
        for i in range(4):
            if i < 2:
                other = jnp.where(nearer(i, 1), block(u, i + 1), block(u, i + 2))
            else:
                other = jnp.where(nearer(i, 0), block(u, i - 1), block(u, i - 2))
            lhs = jnp.concatenate([block(u, i), other], axis=1)
            parts.append(apply(lhs, near_hi[i], near_lo[i]))
        return jnp.concatenate(parts, axis=1)

    def far_product(u, low, high):
        low = jnp.where(g > 0, low, 0.0)
        high = jnp.where(g < GRP - 1, high, 0.0)
        others = [
            jnp.where(nearer(0, 0), block(low, 1), block(low, 0)),
            jnp.where(nearer(1, 0), block(u, 0), block(low, 1)),
            jnp.where(nearer(2, 1), block(u, 3), block(high, 0)),
            jnp.where(nearer(3, 1), block(high, 0), block(high, 1)),
        ]
        return jnp.concatenate(
            [apply(others[i], far_hi[i], far_lo[i]) for i in range(4)], axis=1
        )

    fetches[3].wait()
    load = load_v[...]
    part = load - near_product(u0)
    for copy in halo0:
        copy.wait_recv()
    base = precond * (part - far_product(u0, u_side[0], u_side[1]))
    to_slots(jnp.concatenate([base * sign, precond], axis=0), send2)
    send_parts(1, send2, recv2)
    base_v[...] = base
    halob = send_sides(2, base_v, base_side)

    for copy in halof:
        copy.wait_recv()
    row = lax.broadcasted_iota(i32, (128, DOF // 2), 0)
    for k in range(2):
        slot_side = fixed_side[k, CD : CD + 1, :].astype(i32)
        for m in range(CHIPS):
            slots_side[k, m * 128 : (m + 1) * 128, :] = jnp.where(
                row == slot_side - m * 128, 1.0, 0.0
            ).astype(bf16)

    fetches[9].wait()
    settle(recv1.at[pl.ds(0, PARTS - 1)], recv_sem.at[0])
    settle(recvp, recv_sem.at[2])
    table = recvp[0] + recvp[1] + recvp[2] + recvp[3]
    k_slot = table[:NE]
    s_slot = table[NE:]

    def forces(x, n, high_t, low_t):
        high, low = split2(x)
        high, low = high.astype(bf16), low.astype(bf16)
        move_v[...] = mm(high_t, high) + (mm(low_t, high) + mm(high_t, low))

        def samples(i, force):
            at = pl.multiple_of(8 * i, 8)
            move = move_v[pl.ds(at, 8), :]
            sums = []
            for j in range(8):
                force = jnp.clip(force + k_slot * move[j : j + 1, :], -s_slot, s_slot)
                sums.append(jnp.sum(force, axis=0, keepdims=True))
            total_v[pl.ds(at, 8), :] = jnp.concatenate(sums, axis=0)
            return force

        lax.fori_loop(0, NT // 8, samples, jnp.zeros((NE, 128), f32))
        high, low = split2(total_v[...])
        high, low = high.astype(bf16), low.astype(bf16)
        coefs = mm(basis_v[2], high) + (mm(basis_v[3], high) + mm(basis_v[2], low))
        sendg[n] = coefs.reshape(PARTS, 8, 128)
        for k in (4, 3, 5, 2, 6, 1, 7, 0):
            to = 2 * lax.rem(chip + k, CHIPS) + core
            if n == 0:
                for d, side in enumerate(sides):
                    pltpu.make_async_remote_copy(
                        src_ref=sendg.at[0, to],
                        dst_ref=recvg_side.at[d, chip],
                        send_sem=send_sem.at[5],
                        recv_sem=recv_sem.at[5],
                        device_id=(side, to),
                        device_id_type=MESH,
                    ).start()
            if k > 0:
                pltpu.make_async_remote_copy(
                    src_ref=sendg.at[n, to],
                    dst_ref=recvg.at[n, chip],
                    send_sem=send_sem.at[3 + n],
                    recv_sem=recv_sem.at[3 + n],
                    device_id=(g, to),
                    device_id_type=MESH,
                ).start()
        recvg[n, chip] = sendg[n, h]

    def to_dofs(x, weights):
        lanes = jnp.concatenate([x[m][:CD] for m in range(CHIPS)], axis=1)
        return select3(lanes, weights, mm)

    upper = lax.broadcasted_iota(i32, (1, 8, 128), 1) < CD
    forces(recv1[...].reshape(PARTS * CD, 128), 0, basis_v[4, :, : PARTS * CD], basis_v[5, :, : PARTS * CD])
    settle(recv2.at[pl.ds(0, PARTS - 1)], recv_sem.at[1])
    forces(
        (recv2[...] * jnp.where(upper, 1.0, sendg[0])).reshape(PARTS * 8, 128),
        1,
        basis_v[0],
        basis_v[1],
    )

    settle(recvg.at[0, pl.ds(0, CHIPS - 1)], recv_sem.at[3])
    u1 = base - signed * to_dofs(recvg[0], slots[...])
    part = near_product(u1) + net * u1 - load
    for copy in halob:
        copy.wait_recv()
    settle(recvg_side, recv_sem.at[5])
    low, high = [
        base_side[k] - fixed_side[k, :CD, :] * to_dofs(recvg_side[k], slots_side[k])
        for k in range(2)
    ]
    part = part + far_product(u1, low, high)
    settle(recvg.at[1, pl.ds(0, CHIPS - 1)], recv_sem.at[4])
    residual = part + sign * to_dofs(recvg[1], slots[...])
    out_r[...] = residual
    out_u[...] = u1 - precond * residual

    for copy in halo0 + halof + halob:
        copy.wait_send()
    settle(recv1.at[pl.ds(0, PARTS - 1)], send_sem.at[0])
    settle(recv2.at[pl.ds(0, PARTS - 1)], send_sem.at[1])
    settle(recvp, send_sem.at[2])
    for n in range(2):
        settle(recvg.at[n, pl.ds(0, CHIPS - 1)], send_sem.at[3 + n])
    settle(recvg_side, send_sem.at[5])


def local(u, load, mass, stiffness, offset, dofs, owner, k_table, s_table):
    basis = jnp.asarray(basis_tables())
    hbm = pl.BlockSpec(memory_space=pltpu.HBM)
    vmem = pl.BlockSpec(memory_space=pltpu.VMEM)
    return pl.pallas_call(
        kernel,
        out_shape=[jax.ShapeDtypeStruct((CD, DOF), f32)] * 2,
        in_specs=[hbm] * 10,
        out_specs=[vmem] * 2,
        scratch_shapes=[
            pltpu.VMEM((CD, DOF), f32),
            pltpu.VMEM((CD, DOF), f32),
            pltpu.VMEM((1, DOF), f32),
            pltpu.VMEM((2, 4), i32),
            pltpu.VMEM((1, DOF), i32),
            pltpu.VMEM((1, JOINTS), i32),
            pltpu.VMEM((6, 128, 128), bf16),
            pltpu.VMEM((4, 3, 128, 128), f32),
            pltpu.VMEM((2, 1, NE, GRP * CAP), f32),
            pltpu.VMEM((4, 128, 256), bf16),
            pltpu.VMEM((4, 128, 256), bf16),
            pltpu.VMEM((4, 128, 128), bf16),
            pltpu.VMEM((4, 128, 128), bf16),
            pltpu.VMEM((DOF, DOF), bf16),
            pltpu.VMEM((CHIPS * 128, DOF), bf16),
            pltpu.VMEM((2, CHIPS * 128, DOF // 2), bf16),
            pltpu.VMEM((CHIPS, CD, 128), f32),
            pltpu.VMEM((PARTS, CD, 128), f32),
            pltpu.VMEM((CHIPS, 8, 128), f32),
            pltpu.VMEM((PARTS, 8, 128), f32),
            pltpu.VMEM((4, 2 * NE, 128), f32),
            pltpu.VMEM((4, 2 * NE, 128), f32),
            pltpu.VMEM((NT, 128), f32),
            pltpu.VMEM((NT, 128), f32),
            pltpu.VMEM((2, PARTS, 8, 128), f32),
            pltpu.VMEM((2, CHIPS, 8, 128), f32),
            pltpu.VMEM((2, CHIPS, 8, 128), f32),
            pltpu.VMEM((8, DOF), f32),
            pltpu.VMEM((2, 8, DOF // 2), f32),
            pltpu.VMEM((CD, DOF), f32),
            pltpu.VMEM((2, CD, DOF // 2), f32),
            pltpu.VMEM((2, CD, DOF // 2), f32),
            pltpu.SemaphoreType.DMA((10,)),
            pltpu.SemaphoreType.DMA((6,)),
            pltpu.SemaphoreType.DMA((6,)),
            pltpu.SemaphoreType.DMA((3, 2)),
            pltpu.SemaphoreType.DMA((3, 2)),
        ],
        compiler_params=pltpu.CompilerParams(
            collective_id=0, has_side_effects=True, vmem_limit_bytes=60 * 2**20
        ),
    )(u, load, mass.reshape(1, DOF), offset.T, dofs, owner, basis, stiffness, k_table, s_table)


def solution(mesh):
    in_specs = (
        P("harm", "grp"),
        P("harm", "grp"),
        P("grp"),
        P("grp", None, None, None),
        P("grp", None),
        P("grp", None),
        P("grp", None),
        P("grp", None, None),
        P("grp", None, None),
    )
    out_specs = (P("harm", "grp"), P("harm", "grp"))

    def run(*args):
        return tuple(local(*args))

    return jax.shard_map(run, mesh=mesh, in_specs=in_specs, out_specs=out_specs, check_vma=False)
```

time: 48.9 us -> 37 us (0.76)
  the two profiles are of different devices: /device:TPU:2 before, /device:TPU:1 now
where the time goes in v2:
time: 37 us; the launch traced here: 36.8 us
  Pallas kernels  34.2 us (92%)
  local copies, waits for them, and re-layouts  1.9 us (5%)
  between operations  0.65 us (2%)
    pallas_call x1, Pallas kernels, local(): pl.pallas_call(kernel, out_shape=[jax.ShapeDtypeStruct((CD, DOF), f32)] *...  34.2 us
    unnamed x4, local copies, waits for them, and re-layouts  1.9 us

profile of v2, /device:TPU:1, one launch (start us, length us, event | category | flops | bytes accessed | tf_op | source)
XLA Modules:
  0.0 36.8 jit_solution(9453785552830784907)
XLA Ops:
  0.6 34.2 %shard_map.113 = (f32[4,512]{1,0:T(4,128)}, f32[4,512]{1,0:T(4,128)}) custom-call(f32[4,512]{1,0:T(4,128)} %u_hbm.1, f32[4,512]{1,0:T(4,128)} %load_hbm.1, f32[1,512]{1,0:T(1,128)} %bitcast.2, s32[2,4]{1,0:T(2,128)} %bitcast.3, s32[1,512]{1,0:T(1,128)} %dofs_hbm.1, s32[1,256]{1,0:T(1,128)} %owner_hbm.1, bf16[6,128,128]{2,1,0:T(8,128)(2,1)} %constant.2.clone.basis_hbm, ...), custom_call_target="tpu_custom_call" | custom-call | tf_op jit(solution)/shard_map/pallas_call | solution.py:449
  34.9 0.0 copy-start
  34.9 1.3 %copy.14 = f32[4,512]{1,0:T(4,128)} copy(f32[4,512]{1,0:T(4,128)} %get-tuple-element.4) | data formatting | bytes 16384
  36.2 0.0 copy-done
  36.2 0.6 %copy.15 = f32[4,512]{1,0:T(4,128)} copy(f32[4,512]{1,0:T(4,128)S(1)} %copy-done) | data formatting | bytes 16384
Async XLA Ops:
  34.9 1.3 %copy-start = (f32[4,512]{1,0:T(4,128)S(1)}, f32[4,512]{1,0:T(4,128)}, u32[]{:S(2)}) copy-start(f32[4,512]{1,0:T(4,128)} %get-tuple-element.5) | copy-start | bytes 24580

commit v3 on v2

--- a/solution.py
+++ b/solution.py
@@ -81,8 +81,7 @@
     stiff_hbm,
     k_hbm,
     s_hbm,
-    out_u,
-    out_r,
+    out,
     u_v,
     load_v,
     mass_v,
@@ -209,18 +208,84 @@
     fetches[6].wait()
     fetches[7].wait()
     target = lax.rem(chip + CHIPS - lax.div(g, 4), CHIPS)
-    at = lax.broadcasted_iota(i32, (NE, 128), 1)
-    first = lax.rem(g, 4) * CAP
-    wanted = (at >= first) & (at < first + CAP)
+    at = lax.broadcasted_iota(i32, (8, 128), 1)
+    quarters = [(at >= q * CAP) & (at < (q + 1) * CAP) for q in range(4)]
     for t in range(4):
         column = (target + 8 * t) * CAP
         begin = jnp.minimum(lax.div(column, 128), 4)
-        shift = lax.rem(first - (column - begin * 128) + 512, 256)
-        for a in range(2):
-            part = table_v[a, 0, :, pl.ds(pl.multiple_of(begin * 128, 128), 256)]
-            rolled = pltpu.roll(part, shift, 1)[:, :128]
-            sendp[t, a * NE : (a + 1) * NE, :] = jnp.where(wanted, rolled, 0.0)
-
+        packed = jnp.zeros((8, 128), f32)
+        for q in range(4):
+            rows = pl.ds(8 * (q % 2), 8)
+            part = table_v[q // 2, 0, rows, pl.ds(pl.multiple_of(begin * 128, 128), 256)]
+            shift = lax.rem(q * CAP - (column - begin * 128) + 512, 256)
+            packed = jnp.where(quarters[q], pltpu.roll(part, shift, 1)[:, :128], packed)
+        sendp[t] = packed
+
+    fetches[8].wait()
+    eye = lax.broadcasted_iota(i32, (128, 128), 0) == lax.broadcasted_iota(i32, (128, 128), 1)
+    diagonals = []
+
+    def store(hi, lo, i, at, block):
+        high, low = split2(block)
+        hi[i, :, at : at + 128] = high.astype(bf16)
+        lo[i, :, at : at + 128] = low.astype(bf16)
+
+    for i in range(4):
+        own_block = stiff_v[i, 0]
+        diagonals.append(jnp.sum(jnp.where(eye, own_block, 0.0), axis=0, keepdims=True))
+        store(near_hi, near_lo, i, 0, jnp.where(eye, 0.0, own_block))
+        store(near_hi, near_lo, i, 128, stiff_v[i, 2 if i < 2 else 1])
+        store(far_hi, far_lo, i, 0, stiff_v[i, 1 if i < 2 else 2])
+    kdiag = jnp.concatenate(diagonals, axis=1)
+    coef = 4 * h + lax.broadcasted_iota(i32, (CD, DOF), 0)
+    freq = jnp.where(coef <= HARM, coef, coef - HARM).astype(f32) * (1.0 / HARM)
+    fetches[4].wait()
+    net = kdiag - (freq * freq) * mass_v[...]
+    precond = 1.0 / net
+    signed = precond * sign
+    fixed[...] = jnp.concatenate([signed, jnp.broadcast_to(slot_f, (CD, DOF))], axis=0)
+    fetches[5].wait()
+    offset = offset_v[...]
+
+    def block(u, i):
+        return u[:, i * 128 : (i + 1) * 128]
+
+    def nearer(i, k):
+        return jnp.abs(offset[k : k + 1, i : i + 1]) == 1
+
+    def apply(lhs, hi, lo):
+        terms = terms2(lhs)
+        a = mm_t(terms, hi)
+        b = mm_t(terms, lo)
+        return a[:CD] + (a[CD:] + b[:CD])
+
+    def near_product(u):
+        parts = []
+        for i in range(4):
+            if i < 2:
+                other = jnp.where(nearer(i, 1), block(u, i + 1), block(u, i + 2))
+            else:
+                other = jnp.where(nearer(i, 0), block(u, i - 1), block(u, i - 2))
+            lhs = jnp.concatenate([block(u, i), other], axis=1)
+            parts.append(apply(lhs, near_hi[i], near_lo[i]))
+        return jnp.concatenate(parts, axis=1)
+
+    def far_product(u, low, high):
+        low = jnp.where(g > 0, low, 0.0)
+        high = jnp.where(g < GRP - 1, high, 0.0)
+        others = [
+            jnp.where(nearer(0, 0), block(low, 1), block(low, 0)),
+            jnp.where(nearer(1, 0), block(u, 0), block(low, 1)),
+            jnp.where(nearer(2, 1), block(u, 3), block(high, 0)),
+            jnp.where(nearer(3, 1), block(high, 0), block(high, 1)),
+        ]
+        return jnp.concatenate(
+            [apply(others[i], far_hi[i], far_lo[i]) for i in range(4)], axis=1
+        )
+
+    fetches[3].wait()
+    load = load_v[...]
+    part = load - near_product(u0)
     pl.semaphore_wait(barrier, PARTS - 1 + 2 * CHIPS + 4)
 
     def send_sides(n, src, dst):
@@ -256,6 +321,7 @@
         pltpu.make_async_copy(ref, ref, sem).wait()
 
     halo0 = send_sides(0, u_v, u_side)
+    halof = send_sides(1, fixed, fixed_side)
     for t in range(4):
         pltpu.make_async_remote_copy(
             src_ref=sendp.at[t],
@@ -267,73 +333,7 @@
         ).start()
     send_parts(0, send1, recv1)
 
-    fetches[8].wait()
-    eye = lax.broadcasted_iota(i32, (128, 128), 0) == lax.broadcasted_iota(i32, (128, 128), 1)
-    diagonals = []
-
-    def store(hi, lo, i, at, block):
-        high, low = split2(block)
-        hi[i, :, at : at + 128] = high.astype(bf16)
-        lo[i, :, at : at + 128] = low.astype(bf16)
-
-    for i in range(4):
-        own_block = stiff_v[i, 0]
-        diagonals.append(jnp.sum(jnp.where(eye, own_block, 0.0), axis=0, keepdims=True))
-        store(near_hi, near_lo, i, 0, jnp.where(eye, 0.0, own_block))
-        store(near_hi, near_lo, i, 128, stiff_v[i, 2 if i < 2 else 1])
-        store(far_hi, far_lo, i, 0, stiff_v[i, 1 if i < 2 else 2])
-    kdiag = jnp.concatenate(diagonals, axis=1)
-    coef = 4 * h + lax.broadcasted_iota(i32, (CD, DOF), 0)
-    freq = jnp.where(coef <= HARM, coef, coef - HARM).astype(f32) * (1.0 / HARM)
-    fetches[4].wait()
-    net = kdiag - (freq * freq) * mass_v[...]
-    precond = 1.0 / net
-    signed = precond * sign
-    fixed[...] = jnp.concatenate([signed, jnp.broadcast_to(slot_f, (CD, DOF))], axis=0)
-    halof = send_sides(1, fixed, fixed_side)
-
-    fetches[5].wait()
-    offset = offset_v[...]
-
-    def block(u, i):
-        return u[:, i * 128 : (i + 1) * 128]
-
-    def nearer(i, k):
-        return jnp.abs(offset[k : k + 1, i : i + 1]) == 1
-
-    def apply(lhs, hi, lo):
-        terms = terms2(lhs)
-        a = mm_t(terms, hi)
-        b = mm_t(terms, lo)
-        return a[:CD] + (a[CD:] + b[:CD])
-
-    def near_product(u):
-        parts = []
-        for i in range(4):
-            if i < 2:
-                other = jnp.where(nearer(i, 1), block(u, i + 1), block(u, i + 2))
-            else:
-                other = jnp.where(nearer(i, 0), block(u, i - 1), block(u, i - 2))
-            lhs = jnp.concatenate([block(u, i), other], axis=1)
-            parts.append(apply(lhs, near_hi[i], near_lo[i]))
-        return jnp.concatenate(parts, axis=1)
-
-    def far_product(u, low, high):
-        low = jnp.where(g > 0, low, 0.0)
-        high = jnp.where(g < GRP - 1, high, 0.0)
-        others = [
-            jnp.where(nearer(0, 0), block(low, 1), block(low, 0)),
-            jnp.where(nearer(1, 0), block(u, 0), block(low, 1)),
-            jnp.where(nearer(2, 1), block(u, 3), block(high, 0)),
-            jnp.where(nearer(3, 1), block(high, 0), block(high, 1)),
-        ]
-        return jnp.concatenate(
-            [apply(others[i], far_hi[i], far_lo[i]) for i in range(4)], axis=1
-        )
-
-    fetches[3].wait()
-    load = load_v[...]
-    part = load - near_product(u0)
+
     for copy in halo0:
         copy.wait_recv()
     base = precond * (part - far_product(u0, u_side[0], u_side[1]))
@@ -355,9 +355,17 @@
     fetches[9].wait()
     settle(recv1.at[pl.ds(0, PARTS - 1)], recv_sem.at[0])
     settle(recvp, recv_sem.at[2])
-    table = recvp[0] + recvp[1] + recvp[2] + recvp[3]
-    k_slot = table[:NE]
-    s_slot = table[NE:]
+    table = []
+    for r in range(4):
+        rows = jnp.zeros((8, 128), f32)
+        for q in range(4):
+            part = recvp[q]
+            if q != r:
+                part = pltpu.roll(part, ((q - r) * CAP) % 128, 1)
+            rows = jnp.where(quarters[q], part, rows)
+        table.append(rows)
+    k_slot = jnp.concatenate(table[:2], axis=0)
+    s_slot = jnp.concatenate(table[2:], axis=0)
 
     def forces(x, n, high_t, low_t):
         high, low = split2(x)
@@ -429,8 +437,8 @@
     part = part + far_product(u1, low, high)
     settle(recvg.at[1, pl.ds(0, CHIPS - 1)], recv_sem.at[4])
     residual = part + sign * to_dofs(recvg[1], slots[...])
-    out_r[...] = residual
-    out_u[...] = u1 - precond * residual
+    out[1] = residual
+    out[0] = u1 - precond * residual
 
     for copy in halo0 + halof + halob:
         copy.wait_send()
@@ -446,11 +454,11 @@
     basis = jnp.asarray(basis_tables())
     hbm = pl.BlockSpec(memory_space=pltpu.HBM)
     vmem = pl.BlockSpec(memory_space=pltpu.VMEM)
-    return pl.pallas_call(
+    out = pl.pallas_call(
         kernel,
-        out_shape=[jax.ShapeDtypeStruct((CD, DOF), f32)] * 2,
+        out_shape=pltpu.VMEM((2, CD, DOF), f32),
         in_specs=[hbm] * 10,
-        out_specs=[vmem] * 2,
+        out_specs=vmem,
         scratch_shapes=[
             pltpu.VMEM((CD, DOF), f32),
             pltpu.VMEM((CD, DOF), f32),
@@ -472,8 +480,8 @@
             pltpu.VMEM((PARTS, CD, 128), f32),
             pltpu.VMEM((CHIPS, 8, 128), f32),
             pltpu.VMEM((PARTS, 8, 128), f32),
-            pltpu.VMEM((4, 2 * NE, 128), f32),
-            pltpu.VMEM((4, 2 * NE, 128), f32),
+            pltpu.VMEM((4, 8, 128), f32),
+            pltpu.VMEM((4, 8, 128), f32),
             pltpu.VMEM((NT, 128), f32),
             pltpu.VMEM((NT, 128), f32),
             pltpu.VMEM((2, PARTS, 8, 128), f32),
@@ -494,6 +502,7 @@
             collective_id=0, has_side_effects=True, vmem_limit_bytes=60 * 2**20
         ),
     )(u, load, mass.reshape(1, DOF), offset.T, dofs, owner, basis, stiffness, k_table, s_table)
+    return out[0], out[1]
 
 
 def solution(mesh):

time: 37 us -> 32.4 us (0.88)
  Pallas kernels: 34.2 us -> 31 us
  local copies, waits for them, and re-layouts: 1.9 us -> 0.61 us
    pallas_call x1, Pallas kernels: 34.2 us -> 31 us  [local(): pl.pallas_call(kernel, out_shape=pltpu.VMEM((2, CD, DOF), f32), in_specs=...]
    unnamed x4 -> x0, local copies, waits for them, and re-layouts: 1.9 us -> none
    squeeze x0 -> x1, local copies, waits for them, and re-layouts: none -> 0.61 us  [local(): return (out[0], out[1])]
where the time goes in v3:
time: 32.4 us; the launch traced here: 32.3 us
  Pallas kernels  31 us (96%)
  between operations  0.64 us (2%)
  local copies, waits for them, and re-layouts  0.61 us (2%)
    pallas_call x1, Pallas kernels, local(): pl.pallas_call(kernel, out_shape=pltpu.VMEM((2, CD, DOF), f32), in_specs=...  31 us

profile of v3, /device:TPU:1, one launch (start us, length us, event | category | flops | bytes accessed | tf_op | source)
XLA Modules:
  0.0 32.3 jit_solution(14567921962511923448)
XLA Ops:
  0.6 31.0 %shard_map.113 = f32[2,4,512]{2,1,0:T(4,128)S(1)} custom-call(f32[4,512]{1,0:T(4,128)} %u_hbm.1, f32[4,512]{1,0:T(4,128)} %load_hbm.1, f32[1,512]{1,0:T(1,128)} %bitcast.6, s32[2,4]{1,0:T(2,128)} %bitcast.7, s32[1,512]{1,0:T(1,128)} %dofs_hbm.1, s32[1,256]{1,0:T(1,128)} %owner_hbm.1, bf16[6,128,128]{2,1,0:T(8,128)(2,1)} %constant.2.clone.basis_hbm, ...), custom_call_target="tpu_custom_call" | custom-call | tf_op jit(solution)/shard_map/pallas_call | solution.py:457
  31.7 0.6 %slice_bitcast_fusion = (f32[4,512]{1,0:T(4,128)}, f32[4,512]{1,0:T(4,128)}) fusion(f32[2,4,512]{2,1,0:T(4,128)S(1)} %shard_map.113), kind=kLoop, calls=%fused_computation | loop fusion | bytes 32768 | tf_op jit(solution)/shard_map/squeeze | solution.py:505

commit v4 on v3

--- a/solution.py
+++ b/solution.py
@@ -23,22 +23,20 @@
 
 
 def basis_tables():
-    row = np.arange(PARTS * 8)
-    coef = 4 * (row // 8) + row % 4
+    coef = np.arange(2 * HARM)
     harmonic = np.where(coef <= HARM, coef, coef - HARM)
     angle = 2.0 * math.pi * ((np.arange(NT)[:, None] * harmonic[None, :]) % NT) / NT
     synth = np.where(coef > HARM, np.sin(angle), np.cos(angle))
-    move = (synth - np.roll(synth, 1, axis=0)) * np.where(row % 8 < 4, 1.0, -1.0)
-    project = (synth * np.where(coef == 0, 1.0, 2.0) / NT).T
+    travel = np.zeros((NT, NT), np.float32)
+    travel[:, : 2 * HARM] = synth - synth[-1:]
+    project = np.zeros((NT, NT), np.float32)
+    project[: 2 * HARM] = (synth * np.where(coef == 0, 1.0, 2.0) / NT).T
 
     def split(x):
-        x = x.astype(np.float32)
         high = x.astype(jnp.bfloat16)
         return [high, (x - high.astype(np.float32)).astype(jnp.bfloat16)]
 
-    short = np.zeros((NT, 128))
-    short[:, : PARTS * CD] = move[:, row % 8 < 4]
-    return np.stack(split(move) + split(project) + split(short))
+    return np.stack(split(travel) + split(project))
 
 
 def split2(x):
@@ -104,7 +102,7 @@
     recv2,
     sendp,
     recvp,
-    move_v,
+    travel_v,
     total_v,
     sendg,
     recvg,
@@ -131,7 +129,7 @@
     def greet(group, part):
         pl.semaphore_signal(barrier, inc=1, device_id=(group, part), device_id_type=MESH)
 
-    source = 4 * lax.rem(chip + GRP - g, CHIPS)
+    source = 4 * (chip ^ (g >> 2) ^ 4)
     for k in range(4):
         greet(source + k, 2 * chip + 1 - core)
     for k in (4, 3, 5, 2, 6, 1, 7, 0):
@@ -174,7 +172,7 @@
     )
     earlier = mm(own.astype(bf16), before.astype(bf16))
     rank = jnp.sum(earlier * own, axis=0, keepdims=True)
-    tile = (((owner >> 2) + g) & 7).astype(f32)
+    tile = ((owner >> 2) ^ (g >> 2) ^ 4).astype(f32)
     lane = ((owner & 3) * CAP).astype(f32) + rank
     ones = jnp.ones((1, JOINTS), f32)
     dofs = dofs_v[...]
@@ -201,17 +199,16 @@
     def to_slots(x, out):
         by_slot = select3(x, slots[...], mm_t)
         for m in range(CHIPS):
-            out[m] = by_slot[:, m * 128 : (m + 1) * 128]
-
-    to_slots(u0 * sign, send1)
+            for n in range(x.shape[0] // CD):
+                out[m, n] = by_slot[n * CD : (n + 1) * CD, m * 128 : (m + 1) * 128]
 
     fetches[6].wait()
     fetches[7].wait()
-    target = lax.rem(chip + CHIPS - lax.div(g, 4), CHIPS)
+    target = 4 * (chip ^ (g >> 2) ^ 4)
     at = lax.broadcasted_iota(i32, (8, 128), 1)
     quarters = [(at >= q * CAP) & (at < (q + 1) * CAP) for q in range(4)]
     for t in range(4):
-        column = (target + 8 * t) * CAP
+        column = (target + t) * CAP
         begin = jnp.minimum(lax.div(column, 128), 4)
         packed = jnp.zeros((8, 128), f32)
         for q in range(4):
@@ -243,6 +240,7 @@
     net = kdiag - (freq * freq) * mass_v[...]
     precond = 1.0 / net
     signed = precond * sign
+    to_slots(jnp.concatenate([u0 * sign, precond], axis=0), send1)
     fixed[...] = jnp.concatenate([signed, jnp.broadcast_to(slot_f, (CD, DOF))], axis=0)
     fetches[5].wait()
     offset = offset_v[...]
@@ -321,23 +319,23 @@
         pltpu.make_async_copy(ref, ref, sem).wait()
 
     halo0 = send_sides(0, u_v, u_side)
-    halof = send_sides(1, fixed, fixed_side)
     for t in range(4):
         pltpu.make_async_remote_copy(
             src_ref=sendp.at[t],
             dst_ref=recvp.at[lax.rem(g, 4)],
             send_sem=send_sem.at[2],
             recv_sem=recv_sem.at[2],
-            device_id=(target + 8 * t, 2 * chip + 1 - core),
+            device_id=(target + t, 2 * chip + 1 - core),
             device_id_type=MESH,
         ).start()
     send_parts(0, send1, recv1)
+    halof = send_sides(1, fixed, fixed_side)
 
 
     for copy in halo0:
         copy.wait_recv()
     base = precond * (part - far_product(u0, u_side[0], u_side[1]))
-    to_slots(jnp.concatenate([base * sign, precond], axis=0), send2)
+    to_slots(base * sign, send2)
     send_parts(1, send2, recv2)
     base_v[...] = base
     halob = send_sides(2, base_v, base_side)
@@ -366,27 +364,31 @@
         table.append(rows)
     k_slot = jnp.concatenate(table[:2], axis=0)
     s_slot = jnp.concatenate(table[2:], axis=0)
-
-    def forces(x, n, high_t, low_t):
-        high, low = split2(x)
+    minus_s = -s_slot
+
+    def forces(x, n):
+        high, low = split2(x.reshape(2 * HARM, 128))
         high, low = high.astype(bf16), low.astype(bf16)
-        move_v[...] = mm(high_t, high) + (mm(low_t, high) + mm(high_t, low))
-
-        def samples(i, force):
+        high_t, low_t = basis_v[0, :, : 2 * HARM], basis_v[1, :, : 2 * HARM]
+        travel_v[...] = mm(high_t, high) + (mm(low_t, high) + mm(high_t, low))
+
+        def samples(i, p):
             at = pl.multiple_of(8 * i, 8)
-            move = move_v[pl.ds(at, 8), :]
+            travel = travel_v[pl.ds(at, 8), :]
             sums = []
             for j in range(8):
-                force = jnp.clip(force + k_slot * move[j : j + 1, :], -s_slot, s_slot)
-                sums.append(jnp.sum(force, axis=0, keepdims=True))
+                m = k_slot * travel[j : j + 1, :]
+                p = jnp.minimum(jnp.maximum(p, minus_s - m), s_slot - m)
+                sums.append(jnp.sum(p + m, axis=0, keepdims=True))
             total_v[pl.ds(at, 8), :] = jnp.concatenate(sums, axis=0)
-            return force
-
-        lax.fori_loop(0, NT // 8, samples, jnp.zeros((NE, 128), f32))
+            return p
+
+        lax.fori_loop(0, NT // 8, samples, jnp.zeros((NE, 128), f32), unroll=4)
         high, low = split2(total_v[...])
         high, low = high.astype(bf16), low.astype(bf16)
-        coefs = mm(basis_v[2], high) + (mm(basis_v[3], high) + mm(basis_v[2], low))
-        sendg[n] = coefs.reshape(PARTS, 8, 128)
+        high_t, low_t = basis_v[2, : 2 * HARM], basis_v[3, : 2 * HARM]
+        coefs = mm(high_t, high) + (mm(low_t, high) + mm(high_t, low))
+        sendg[n] = coefs.reshape(PARTS, CD, 128)
         for k in (4, 3, 5, 2, 6, 1, 7, 0):
             to = 2 * lax.rem(chip + k, CHIPS) + core
             if n == 0:
@@ -411,18 +413,12 @@
         recvg[n, chip] = sendg[n, h]
 
     def to_dofs(x, weights):
-        lanes = jnp.concatenate([x[m][:CD] for m in range(CHIPS)], axis=1)
+        lanes = jnp.concatenate([x[m] for m in range(CHIPS)], axis=1)
         return select3(lanes, weights, mm)
 
-    upper = lax.broadcasted_iota(i32, (1, 8, 128), 1) < CD
-    forces(recv1[...].reshape(PARTS * CD, 128), 0, basis_v[4, :, : PARTS * CD], basis_v[5, :, : PARTS * CD])
+    forces(recv1[:, 0], 0)
     settle(recv2.at[pl.ds(0, PARTS - 1)], recv_sem.at[1])
-    forces(
-        (recv2[...] * jnp.where(upper, 1.0, sendg[0])).reshape(PARTS * 8, 128),
-        1,
-        basis_v[0],
-        basis_v[1],
-    )
+    forces(recv2[:, 0] - recv1[:, 1] * sendg[0], 1)
 
     settle(recvg.at[0, pl.ds(0, CHIPS - 1)], recv_sem.at[3])
     u1 = base - signed * to_dofs(recvg[0], slots[...])
@@ -466,7 +462,7 @@
             pltpu.VMEM((2, 4), i32),
             pltpu.VMEM((1, DOF), i32),
             pltpu.VMEM((1, JOINTS), i32),
-            pltpu.VMEM((6, 128, 128), bf16),
+            pltpu.VMEM((4, 128, 128), bf16),
             pltpu.VMEM((4, 3, 128, 128), f32),
             pltpu.VMEM((2, 1, NE, GRP * CAP), f32),
             pltpu.VMEM((4, 128, 256), bf16),
@@ -476,17 +472,17 @@
             pltpu.VMEM((DOF, DOF), bf16),
             pltpu.VMEM((CHIPS * 128, DOF), bf16),
             pltpu.VMEM((2, CHIPS * 128, DOF // 2), bf16),
-            pltpu.VMEM((CHIPS, CD, 128), f32),
-            pltpu.VMEM((PARTS, CD, 128), f32),
-            pltpu.VMEM((CHIPS, 8, 128), f32),
-            pltpu.VMEM((PARTS, 8, 128), f32),
+            pltpu.VMEM((CHIPS, 2, CD, 128), f32),
+            pltpu.VMEM((PARTS, 2, CD, 128), f32),
+            pltpu.VMEM((CHIPS, 1, CD, 128), f32),
+            pltpu.VMEM((PARTS, 1, CD, 128), f32),
             pltpu.VMEM((4, 8, 128), f32),
             pltpu.VMEM((4, 8, 128), f32),
             pltpu.VMEM((NT, 128), f32),
             pltpu.VMEM((NT, 128), f32),
-            pltpu.VMEM((2, PARTS, 8, 128), f32),
-            pltpu.VMEM((2, CHIPS, 8, 128), f32),
-            pltpu.VMEM((2, CHIPS, 8, 128), f32),
+            pltpu.VMEM((2, PARTS, CD, 128), f32),
+            pltpu.VMEM((2, CHIPS, CD, 128), f32),
+            pltpu.VMEM((2, CHIPS, CD, 128), f32),
             pltpu.VMEM((8, DOF), f32),
             pltpu.VMEM((2, 8, DOF // 2), f32),
             pltpu.VMEM((CD, DOF), f32),

time: 32.4 us -> 32 us (0.988)
  Pallas kernels: 31 us -> 30.6 us
    pallas_call x1, Pallas kernels: 31 us -> 30.6 us  [local(): pl.pallas_call(kernel, out_shape=pltpu.VMEM((2, CD, DOF), f32), in_specs=...]
where the time goes in v4:
time: 32 us; the launch traced here: 31.8 us
  Pallas kernels  30.6 us (96%)
  between operations  0.64 us (2%)
  local copies, waits for them, and re-layouts  0.61 us (2%)
    pallas_call x1, Pallas kernels, local(): pl.pallas_call(kernel, out_shape=pltpu.VMEM((2, CD, DOF), f32), in_specs=...  30.6 us

profile of v4, /device:TPU:1, one launch (start us, length us, event | category | flops | bytes accessed | tf_op | source)
XLA Modules:
  0.0 31.8 jit_solution(17013143978038673448)
XLA Ops:
  0.6 30.6 %shard_map.113 = f32[2,4,512]{2,1,0:T(4,128)S(1)} custom-call(f32[4,512]{1,0:T(4,128)} %u_hbm.1, f32[4,512]{1,0:T(4,128)} %load_hbm.1, f32[1,512]{1,0:T(1,128)} %bitcast.6, s32[2,4]{1,0:T(2,128)} %bitcast.7, s32[1,512]{1,0:T(1,128)} %dofs_hbm.1, s32[1,256]{1,0:T(1,128)} %owner_hbm.1, bf16[4,128,128]{2,1,0:T(8,128)(2,1)} %constant.2.clone.basis_hbm, ...), custom_call_target="tpu_custom_call" | custom-call | tf_op jit(solution)/shard_map/pallas_call | solution.py:453
  31.2 0.6 %slice_bitcast_fusion = (f32[4,512]{1,0:T(4,128)}, f32[4,512]{1,0:T(4,128)}) fusion(f32[2,4,512]{2,1,0:T(4,128)S(1)} %shard_map.113), kind=kLoop, calls=%fused_computation | loop fusion | bytes 32768 | tf_op jit(solution)/shard_map/squeeze | solution.py:501

commit v5 on v4

--- a/solution.py
+++ b/solution.py
@@ -117,6 +117,7 @@
     recv_sem,
     side_send,
     side_recv,
+    ready,
 ):
     g = lax.axis_index("grp")
     h = lax.axis_index("harm")
@@ -124,21 +125,49 @@
     core = lax.rem(h, 2)
     sides = (lax.rem(g + 1, GRP), lax.rem(g + GRP - 1, GRP))
 
+    far = [(4 * (chip ^ (g >> 2) ^ 4) + t, 2 * chip + 1 - core) for t in range(4)]
+
+    def place(part):
+        y = part >> 1
+        return 2 * jnp.where(y < 4, y, 11 - y) + (part & 1)
+
+    def far_place(group, part):
+        return 8 * (group & 7) + 2 * (group >> 3) + (part & 1)
+
+    mates = [lax.rem(h + k, PARTS) for k in (8, 7, 9, 6, 10, 5, 11, 4, 12, 3, 13, 2, 14, 1, 15)]
+    later_mate = [place(part) > place(h) for part in mates]
+    exists = (g < GRP - 1, g > 0)
+    later_side = [there & ((side & 7) > (g & 7)) for there, side in zip(exists, sides)]
+    earlier_side = [there & ((side & 7) < (g & 7)) for there, side in zip(exists, sides)]
+    later_far = [far_place(*peer) > far_place(g, h) for peer in far]
+    n_mates = PARTS - 1 - place(h)
+    n_sides = sum(later.astype(i32) for later in later_side)
+    n_before = sum(earlier.astype(i32) for earlier in earlier_side)
+    n_far = sum(later.astype(i32) for later in later_far)
     barrier = pltpu.get_barrier_semaphore()
 
-    def greet(group, part):
-        pl.semaphore_signal(barrier, inc=1, device_id=(group, part), device_id_type=MESH)
-
-    source = 4 * (chip ^ (g >> 2) ^ 4)
-    for k in range(4):
-        greet(source + k, 2 * chip + 1 - core)
-    for k in (4, 3, 5, 2, 6, 1, 7, 0):
-        part = 2 * lax.rem(chip + k, CHIPS)
-        for side in sides:
-            greet(side, part + core)
-        if k > 0:
-            greet(g, part + core)
-        greet(g, part + 1 - core)
+    def signal(sem, group, part):
+        pl.semaphore_signal(sem, inc=1, device_id=(group, part), device_id_type=MESH)
+
+    def tell(later, sems):
+        def when(flag, peers, sem):
+            @pl.when(flag)
+            def _():
+                for group, part in peers:
+                    signal(sem, group, part)
+
+        side_flags = later_side if later else earlier_side
+        for d, side in enumerate(sides):
+            when(side_flags[d], [(side, h)], sems[1])
+        for flag, peer in zip(later_far, far):
+            when(flag if later else jnp.logical_not(flag), [peer], sems[2])
+        for flag, part in zip(later_mate, mates):
+            when(flag if later else jnp.logical_not(flag), [(g, part)], sems[0])
+        for d, side in enumerate(sides):
+            others = [(side, 2 * lax.rem(chip + k, CHIPS) + core) for k in (4, 3, 5, 2, 6, 1, 7)]
+            when(side_flags[d], others, sems[3])
+
+    tell(True, [barrier] * 4)
 
     fetches = [
         pltpu.make_async_copy(src, dst, local_sem.at[i])
@@ -159,6 +188,72 @@
     ]
     for fetch in fetches:
         fetch.start()
+
+    def await_some(sem, n):
+        @pl.when(n > 0)
+        def _():
+            pl.semaphore_wait(sem, n)
+
+    await_some(barrier, (PARTS - 1 - n_mates) + CHIPS * n_before + (4 - n_far))
+    tell(False, [ready.at[i] for i in range(4)])
+
+    def start_if(copies, flags):
+        for copy, flag in zip(copies, flags):
+            pl.when(flag)(copy.start)
+
+    def wait_sides(copies):
+        for copy, there in zip(copies, (g > 0, g < GRP - 1)):
+            pl.when(there)(copy.wait_recv)
+
+    for k, there in enumerate((g > 0, g < GRP - 1)):
+
+        @pl.when(jnp.logical_not(there))
+        def _():
+            for ref in (u_side, fixed_side, base_side, recvg_side):
+                ref[k] = jnp.zeros(ref.shape[1:], f32)
+
+    def side_copies(n, src, dst):
+        return [
+            pltpu.make_async_remote_copy(
+                src_ref=src.at[:, 256:512] if k == 0 else src.at[:, 0:256],
+                dst_ref=dst.at[k],
+                send_sem=side_send.at[n, k],
+                recv_sem=side_recv.at[n, k],
+                device_id=(side, h),
+                device_id_type=MESH,
+            )
+            for k, side in enumerate(sides)
+        ]
+
+    def send_sides(n, src, dst):
+        copies = side_copies(n, src, dst)
+        start_if(copies, exists)
+        return copies
+
+    def send_parts(n, src, dst):
+        for to in mates:
+            pltpu.make_async_remote_copy(
+                src_ref=src.at[lax.div(to, 2)],
+                dst_ref=dst.at[h],
+                send_sem=send_sem.at[n],
+                recv_sem=recv_sem.at[n],
+                device_id=(g, to),
+                device_id_type=MESH,
+            ).start()
+        dst[h] = src[chip]
+
+    def settle(ref, sem):
+        pltpu.make_async_copy(ref, ref, sem).wait()
+
+    def settle_sides(sems, flags):
+        for d, there in enumerate(flags):
+
+            @pl.when(there)
+            def _():
+                settle(recvg_side.at[d], sems.at[5 + d])
+
+    halo0 = side_copies(0, u_hbm, u_side)
+    start_if(halo0, earlier_side)
 
     fetches[0].wait()
     fetches[1].wait()
@@ -204,11 +299,10 @@
 
     fetches[6].wait()
     fetches[7].wait()
-    target = 4 * (chip ^ (g >> 2) ^ 4)
     at = lax.broadcasted_iota(i32, (8, 128), 1)
     quarters = [(at >= q * CAP) & (at < (q + 1) * CAP) for q in range(4)]
     for t in range(4):
-        column = (target + t) * CAP
+        column = far[t][0] * CAP
         begin = jnp.minimum(lax.div(column, 128), 4)
         packed = jnp.zeros((8, 128), f32)
         for q in range(4):
@@ -217,6 +311,18 @@
             shift = lax.rem(q * CAP - (column - begin * 128) + 512, 256)
             packed = jnp.where(quarters[q], pltpu.roll(part, shift, 1)[:, :128], packed)
         sendp[t] = packed
+    tables = [
+        pltpu.make_async_remote_copy(
+            src_ref=sendp.at[t],
+            dst_ref=recvp.at[lax.rem(g, 4)],
+            send_sem=send_sem.at[2],
+            recv_sem=recv_sem.at[2],
+            device_id=peer,
+            device_id_type=MESH,
+        )
+        for t, peer in enumerate(far)
+    ]
+    start_if(tables, [jnp.logical_not(later) for later in later_far])
 
     fetches[8].wait()
     eye = lax.broadcasted_iota(i32, (128, 128), 0) == lax.broadcasted_iota(i32, (128, 128), 1)
@@ -269,8 +375,6 @@
         return jnp.concatenate(parts, axis=1)
 
     def far_product(u, low, high):
-        low = jnp.where(g > 0, low, 0.0)
-        high = jnp.where(g < GRP - 1, high, 0.0)
         others = [
             jnp.where(nearer(0, 0), block(low, 1), block(low, 0)),
             jnp.where(nearer(1, 0), block(u, 0), block(low, 1)),
@@ -284,71 +388,21 @@
     fetches[3].wait()
     load = load_v[...]
     part = load - near_product(u0)
-    pl.semaphore_wait(barrier, PARTS - 1 + 2 * CHIPS + 4)
-
-    def send_sides(n, src, dst):
-        copies = [
-            pltpu.make_async_remote_copy(
-                src_ref=src.at[:, 256:512] if k == 0 else src.at[:, 0:256],
-                dst_ref=dst.at[k],
-                send_sem=side_send.at[n, k],
-                recv_sem=side_recv.at[n, k],
-                device_id=(side, h),
-                device_id_type=MESH,
-            )
-            for k, side in enumerate(sides)
-        ]
-        for copy in copies:
-            copy.start()
-        return copies
-
-    def send_parts(n, src, dst):
-        for k in (8, 7, 9, 6, 10, 5, 11, 4, 12, 3, 13, 2, 14, 1, 15):
-            to = lax.rem(h + k, PARTS)
-            pltpu.make_async_remote_copy(
-                src_ref=src.at[lax.div(to, 2)],
-                dst_ref=dst.at[h],
-                send_sem=send_sem.at[n],
-                recv_sem=recv_sem.at[n],
-                device_id=(g, to),
-                device_id_type=MESH,
-            ).start()
-        dst[h] = src[chip]
-
-    def settle(ref, sem):
-        pltpu.make_async_copy(ref, ref, sem).wait()
-
-    halo0 = send_sides(0, u_v, u_side)
-    for t in range(4):
-        pltpu.make_async_remote_copy(
-            src_ref=sendp.at[t],
-            dst_ref=recvp.at[lax.rem(g, 4)],
-            send_sem=send_sem.at[2],
-            recv_sem=recv_sem.at[2],
-            device_id=(target + t, 2 * chip + 1 - core),
-            device_id_type=MESH,
-        ).start()
+    await_some(ready.at[0], n_mates)
     send_parts(0, send1, recv1)
+    await_some(ready.at[1], n_sides)
+    start_if(halo0, later_side)
     halof = send_sides(1, fixed, fixed_side)
-
-
-    for copy in halo0:
-        copy.wait_recv()
+    await_some(ready.at[2], n_far)
+    start_if(tables, later_far)
+
+
+    wait_sides(halo0)
     base = precond * (part - far_product(u0, u_side[0], u_side[1]))
     to_slots(base * sign, send2)
     send_parts(1, send2, recv2)
     base_v[...] = base
     halob = send_sides(2, base_v, base_side)
-
-    for copy in halof:
-        copy.wait_recv()
-    row = lax.broadcasted_iota(i32, (128, DOF // 2), 0)
-    for k in range(2):
-        slot_side = fixed_side[k, CD : CD + 1, :].astype(i32)
-        for m in range(CHIPS):
-            slots_side[k, m * 128 : (m + 1) * 128, :] = jnp.where(
-                row == slot_side - m * 128, 1.0, 0.0
-            ).astype(bf16)
 
     fetches[9].wait()
     settle(recv1.at[pl.ds(0, PARTS - 1)], recv_sem.at[0])
@@ -389,18 +443,23 @@
         high_t, low_t = basis_v[2, : 2 * HARM], basis_v[3, : 2 * HARM]
         coefs = mm(high_t, high) + (mm(low_t, high) + mm(high_t, low))
         sendg[n] = coefs.reshape(PARTS, CD, 128)
+        if n == 0:
+            await_some(ready.at[3], (CHIPS - 1) * n_sides)
         for k in (4, 3, 5, 2, 6, 1, 7, 0):
             to = 2 * lax.rem(chip + k, CHIPS) + core
             if n == 0:
-                for d, side in enumerate(sides):
+                copies = [
                     pltpu.make_async_remote_copy(
                         src_ref=sendg.at[0, to],
                         dst_ref=recvg_side.at[d, chip],
-                        send_sem=send_sem.at[5],
-                        recv_sem=recv_sem.at[5],
+                        send_sem=send_sem.at[5 + d],
+                        recv_sem=recv_sem.at[5 + d],
                         device_id=(side, to),
                         device_id_type=MESH,
-                    ).start()
+                    )
+                    for d, side in enumerate(sides)
+                ]
+                start_if(copies, exists)
             if k > 0:
                 pltpu.make_async_remote_copy(
                     src_ref=sendg.at[n, to],
@@ -420,12 +479,20 @@
     settle(recv2.at[pl.ds(0, PARTS - 1)], recv_sem.at[1])
     forces(recv2[:, 0] - recv1[:, 1] * sendg[0], 1)
 
+    wait_sides(halof)
+    row = lax.broadcasted_iota(i32, (128, DOF // 2), 0)
+    for k in range(2):
+        slot_side = fixed_side[k, CD : CD + 1, :].astype(i32)
+        for m in range(CHIPS):
+            slots_side[k, m * 128 : (m + 1) * 128, :] = jnp.where(
+                row == slot_side - m * 128, 1.0, 0.0
+            ).astype(bf16)
+
     settle(recvg.at[0, pl.ds(0, CHIPS - 1)], recv_sem.at[3])
     u1 = base - signed * to_dofs(recvg[0], slots[...])
     part = near_product(u1) + net * u1 - load
-    for copy in halob:
-        copy.wait_recv()
-    settle(recvg_side, recv_sem.at[5])
+    wait_sides(halob)
+    settle_sides(recv_sem, (g > 0, g < GRP - 1))
     low, high = [
         base_side[k] - fixed_side[k, :CD, :] * to_dofs(recvg_side[k], slots_side[k])
         for k in range(2)
@@ -436,14 +503,15 @@
     out[1] = residual
     out[0] = u1 - precond * residual
 
-    for copy in halo0 + halof + halob:
-        copy.wait_send()
+    for copies in (halo0, halof, halob):
+        for copy, there in zip(copies, exists):
+            pl.when(there)(copy.wait_send)
     settle(recv1.at[pl.ds(0, PARTS - 1)], send_sem.at[0])
     settle(recv2.at[pl.ds(0, PARTS - 1)], send_sem.at[1])
     settle(recvp, send_sem.at[2])
     for n in range(2):
         settle(recvg.at[n, pl.ds(0, CHIPS - 1)], send_sem.at[3 + n])
-    settle(recvg_side, send_sem.at[5])
+    settle_sides(send_sem, exists)
 
 
 def local(u, load, mass, stiffness, offset, dofs, owner, k_table, s_table):
@@ -489,10 +557,11 @@
             pltpu.VMEM((2, CD, DOF // 2), f32),
             pltpu.VMEM((2, CD, DOF // 2), f32),
             pltpu.SemaphoreType.DMA((10,)),
-            pltpu.SemaphoreType.DMA((6,)),
-            pltpu.SemaphoreType.DMA((6,)),
+            pltpu.SemaphoreType.DMA((7,)),
+            pltpu.SemaphoreType.DMA((7,)),
             pltpu.SemaphoreType.DMA((3, 2)),
             pltpu.SemaphoreType.DMA((3, 2)),
+            pltpu.SemaphoreType.REGULAR((4,)),
         ],
         compiler_params=pltpu.CompilerParams(
             collective_id=0, has_side_effects=True, vmem_limit_bytes=60 * 2**20

time: 32 us -> 30.6 us (0.956)
  the two profiles are of different devices: /device:TPU:1 before, /device:TPU:6 now
where the time goes in v5:
time: 30.6 us; the launch traced here: 30.4 us
  Pallas kernels  29.2 us (95%)
  between operations  0.64 us (2%)
  local copies, waits for them, and re-layouts  0.61 us (2%)
    pallas_call x1, Pallas kernels, local(): pl.pallas_call(kernel, out_shape=pltpu.VMEM((2, CD, DOF), f32), in_specs=...  29.2 us

profile of v5, /device:TPU:6, one launch (start us, length us, event | category | flops | bytes accessed | tf_op | source)
XLA Modules:
  0.0 30.4 jit_solution(10113270808441359590)
XLA Ops:
  0.6 29.2 %shard_map.113 = f32[2,4,512]{2,1,0:T(4,128)S(1)} custom-call(f32[4,512]{1,0:T(4,128)} %u_hbm.1, f32[4,512]{1,0:T(4,128)} %load_hbm.1, f32[1,512]{1,0:T(1,128)} %bitcast.6, s32[2,4]{1,0:T(2,128)} %bitcast.7, s32[1,512]{1,0:T(1,128)} %dofs_hbm.1, s32[1,256]{1,0:T(1,128)} %owner_hbm.1, bf16[4,128,128]{2,1,0:T(8,128)(2,1)} %constant.2.clone.basis_hbm, ...), custom_call_target="tpu_custom_call" | custom-call | tf_op jit(solution)/shard_map/pallas_call | solution.py:521
  29.8 0.6 %slice_bitcast_fusion = (f32[4,512]{1,0:T(4,128)}, f32[4,512]{1,0:T(4,128)}) fusion(f32[2,4,512]{2,1,0:T(4,128)S(1)} %shard_map.113), kind=kLoop, calls=%fused_computation | loop fusion | bytes 32768 | tf_op jit(solution)/shard_map/squeeze | solution.py:570

commit v6 on v5

--- a/solution.py
+++ b/solution.py
@@ -135,7 +135,6 @@
         return 8 * (group & 7) + 2 * (group >> 3) + (part & 1)
 
     mates = [lax.rem(h + k, PARTS) for k in (8, 7, 9, 6, 10, 5, 11, 4, 12, 3, 13, 2, 14, 1, 15)]
-    later_mate = [place(part) > place(h) for part in mates]
     exists = (g < GRP - 1, g > 0)
     later_side = [there & ((side & 7) > (g & 7)) for there, side in zip(exists, sides)]
     earlier_side = [there & ((side & 7) < (g & 7)) for there, side in zip(exists, sides)]
@@ -157,17 +156,51 @@
                     signal(sem, group, part)
 
         side_flags = later_side if later else earlier_side
-        for d, side in enumerate(sides):
-            when(side_flags[d], [(side, h)], sems[1])
         for flag, peer in zip(later_far, far):
             when(flag if later else jnp.logical_not(flag), [peer], sems[2])
-        for flag, part in zip(later_mate, mates):
-            when(flag if later else jnp.logical_not(flag), [(g, part)], sems[0])
+        for d, side in enumerate(sides):
+            when(side_flags[d], [(side, h)], sems[5 - d])
+
+        def mate(p, _):
+            y = p >> 1
+            signal(sems[0], g, 2 * jnp.where(y < 4, y, 11 - y) + (p & 1))
+            return 0
+
+        mine = place(h)
+        lax.fori_loop(mine + 1 if later else 0, PARTS if later else mine, mate, 0)
         for d, side in enumerate(sides):
             others = [(side, 2 * lax.rem(chip + k, CHIPS) + core) for k in (4, 3, 5, 2, 6, 1, 7)]
             when(side_flags[d], others, sems[3])
 
-    tell(True, [barrier] * 4)
+    tell(True, [barrier] * 6)
+
+    def await_some(sem, n):
+        @pl.when(n > 0)
+        def _():
+            pl.semaphore_wait(sem, n)
+
+    await_some(barrier, (PARTS - 1 - n_mates) + CHIPS * n_before + (4 - n_far))
+    def side_copies(n, src, dst):
+        return [
+            pltpu.make_async_remote_copy(
+                src_ref=src.at[:, 256:512] if k == 0 else src.at[:, 0:256],
+                dst_ref=dst.at[k],
+                send_sem=side_send.at[n, k],
+                recv_sem=side_recv.at[n, k],
+                device_id=(side, h),
+                device_id_type=MESH,
+            )
+            for k, side in enumerate(sides)
+        ]
+
+    def start_if(copies, flags):
+        for copy, flag in zip(copies, flags):
+            pl.when(flag)(copy.start)
+
+    halo0 = side_copies(0, u_hbm, u_side)
+    start_if(halo0, earlier_side)
+
+    tell(False, [ready.at[i] for i in range(6)])
 
     fetches = [
         pltpu.make_async_copy(src, dst, local_sem.at[i])
@@ -189,18 +222,6 @@
     for fetch in fetches:
         fetch.start()
 
-    def await_some(sem, n):
-        @pl.when(n > 0)
-        def _():
-            pl.semaphore_wait(sem, n)
-
-    await_some(barrier, (PARTS - 1 - n_mates) + CHIPS * n_before + (4 - n_far))
-    tell(False, [ready.at[i] for i in range(4)])
-
-    def start_if(copies, flags):
-        for copy, flag in zip(copies, flags):
-            pl.when(flag)(copy.start)
-
     def wait_sides(copies):
         for copy, there in zip(copies, (g > 0, g < GRP - 1)):
             pl.when(there)(copy.wait_recv)
@@ -211,19 +232,6 @@
         def _():
             for ref in (u_side, fixed_side, base_side, recvg_side):
                 ref[k] = jnp.zeros(ref.shape[1:], f32)
-
-    def side_copies(n, src, dst):
-        return [
-            pltpu.make_async_remote_copy(
-                src_ref=src.at[:, 256:512] if k == 0 else src.at[:, 0:256],
-                dst_ref=dst.at[k],
-                send_sem=side_send.at[n, k],
-                recv_sem=side_recv.at[n, k],
-                device_id=(side, h),
-                device_id_type=MESH,
-            )
-            for k, side in enumerate(sides)
-        ]
 
     def send_sides(n, src, dst):
         copies = side_copies(n, src, dst)
@@ -251,9 +259,6 @@
             @pl.when(there)
             def _():
                 settle(recvg_side.at[d], sems.at[5 + d])
-
-    halo0 = side_copies(0, u_hbm, u_side)
-    start_if(halo0, earlier_side)
 
     fetches[0].wait()
     fetches[1].wait()
@@ -388,19 +393,29 @@
     fetches[3].wait()
     load = load_v[...]
     part = load - near_product(u0)
+    def halo_later(d):
+        @pl.when(later_side[d])
+        def _():
+            pl.semaphore_wait(ready.at[4 + d], 1)
+            halo0[d].start()
+
+    halo_later(0)
     await_some(ready.at[0], n_mates)
     send_parts(0, send1, recv1)
-    await_some(ready.at[1], n_sides)
-    start_if(halo0, later_side)
+    halo_later(1)
     halof = send_sides(1, fixed, fixed_side)
-    await_some(ready.at[2], n_far)
-    start_if(tables, later_far)
+    def tables_later(now):
+        await_some(ready.at[2], jnp.where(now, n_far, 0))
+        start_if(tables, [now & later for later in later_far])
+
+    tables_later((g & 7) > 0)
 
 
     wait_sides(halo0)
     base = precond * (part - far_product(u0, u_side[0], u_side[1]))
     to_slots(base * sign, send2)
     send_parts(1, send2, recv2)
+    tables_later((g & 7) == 0)
     base_v[...] = base
     halob = send_sides(2, base_v, base_side)
 
@@ -492,14 +507,14 @@
     u1 = base - signed * to_dofs(recvg[0], slots[...])
     part = near_product(u1) + net * u1 - load
     wait_sides(halob)
+    settle(recvg.at[1, pl.ds(0, CHIPS - 1)], recv_sem.at[4])
+    part = part + sign * to_dofs(recvg[1], slots[...])
     settle_sides(recv_sem, (g > 0, g < GRP - 1))
     low, high = [
         base_side[k] - fixed_side[k, :CD, :] * to_dofs(recvg_side[k], slots_side[k])
         for k in range(2)
     ]
-    part = part + far_product(u1, low, high)
-    settle(recvg.at[1, pl.ds(0, CHIPS - 1)], recv_sem.at[4])
-    residual = part + sign * to_dofs(recvg[1], slots[...])
+    residual = part + far_product(u1, low, high)
     out[1] = residual
     out[0] = u1 - precond * residual
 
@@ -561,7 +576,7 @@
             pltpu.SemaphoreType.DMA((7,)),
             pltpu.SemaphoreType.DMA((3, 2)),
             pltpu.SemaphoreType.DMA((3, 2)),
-            pltpu.SemaphoreType.REGULAR((4,)),
+            pltpu.SemaphoreType.REGULAR((6,)),
         ],
         compiler_params=pltpu.CompilerParams(
             collective_id=0, has_side_effects=True, vmem_limit_bytes=60 * 2**20

time: 30.6 us -> 30.6 us (level)
  no operation moved by 1% of the time
where the time goes in v6:
time: 30.6 us; the launch traced here: 30.5 us
  Pallas kernels  29.3 us (96%)
  between operations  0.64 us (2%)
  local copies, waits for them, and re-layouts  0.61 us (2%)
    pallas_call x1, Pallas kernels, local(): pl.pallas_call(kernel, out_shape=pltpu.VMEM((2, CD, DOF), f32), in_specs=...  29.3 us

profile of v6, /device:TPU:6, one launch (start us, length us, event | category | flops | bytes accessed | tf_op | source)
XLA Modules:
  0.0 30.5 jit_solution(15204266448958311610)
XLA Ops:
  0.6 29.3 %shard_map.113 = f32[2,4,512]{2,1,0:T(4,128)S(1)} custom-call(f32[4,512]{1,0:T(4,128)} %u_hbm.1, f32[4,512]{1,0:T(4,128)} %load_hbm.1, f32[1,512]{1,0:T(1,128)} %bitcast.6, s32[2,4]{1,0:T(2,128)} %bitcast.7, s32[1,512]{1,0:T(1,128)} %dofs_hbm.1, s32[1,256]{1,0:T(1,128)} %owner_hbm.1, bf16[4,128,128]{2,1,0:T(8,128)(2,1)} %constant.2.clone.basis_hbm, ...), custom_call_target="tpu_custom_call" | custom-call | tf_op jit(solution)/shard_map/pallas_call | solution.py:536
  29.9 0.6 %slice_bitcast_fusion = (f32[4,512]{1,0:T(4,128)}, f32[4,512]{1,0:T(4,128)}) fusion(f32[2,4,512]{2,1,0:T(4,128)S(1)} %shard_map.113), kind=kLoop, calls=%fused_computation | loop fusion | bytes 32768 | tf_op jit(solution)/shard_map/squeeze | solution.py:585

commit v7 on v6

--- a/solution.py
+++ b/solution.py
@@ -48,12 +48,6 @@
     return jnp.concatenate(split2(x), axis=0).astype(bf16)
 
 
-def terms3(x):
-    high, rest = split2(x)
-    mid, low = split2(rest)
-    return jnp.concatenate([high, mid, low], axis=0).astype(bf16)
-
-
 def mm(a, b):
     return lax.dot_general(a, b, (((1,), (0,)), ((), ())), preferred_element_type=f32)
 
@@ -62,10 +56,10 @@
     return lax.dot_general(a, b, (((1,), (1,)), ((), ())), preferred_element_type=f32)
 
 
-def select3(x, weights, product):
+def select2(x, weights, product):
     n = x.shape[0]
-    y = product(terms3(x), weights)
-    return y[:n] + y[n : 2 * n] + y[2 * n :]
+    y = product(terms2(x), weights)
+    return y[:n] + y[n:]
 
 
 def kernel(
@@ -297,7 +291,7 @@
     u0 = u_v[...]
 
     def to_slots(x, out):
-        by_slot = select3(x, slots[...], mm_t)
+        by_slot = select2(x, slots[...], mm_t)
         for m in range(CHIPS):
             for n in range(x.shape[0] // CD):
                 out[m, n] = by_slot[n * CD : (n + 1) * CD, m * 128 : (m + 1) * 128]
@@ -452,7 +446,7 @@
             total_v[pl.ds(at, 8), :] = jnp.concatenate(sums, axis=0)
             return p
 
-        lax.fori_loop(0, NT // 8, samples, jnp.zeros((NE, 128), f32), unroll=4)
+        lax.fori_loop(0, NT // 8, samples, jnp.zeros((NE, 128), f32), unroll=16)
         high, low = split2(total_v[...])
         high, low = high.astype(bf16), low.astype(bf16)
         high_t, low_t = basis_v[2, : 2 * HARM], basis_v[3, : 2 * HARM]
@@ -488,7 +482,7 @@
 
     def to_dofs(x, weights):
         lanes = jnp.concatenate([x[m] for m in range(CHIPS)], axis=1)
-        return select3(lanes, weights, mm)
+        return select2(lanes, weights, mm)
 
     forces(recv1[:, 0], 0)
     settle(recv2.at[pl.ds(0, PARTS - 1)], recv_sem.at[1])

time: 30.6 us -> 30.6 us (level)
  no operation moved by 1% of the time
where the time goes in v7:
time: 30.6 us; the launch traced here: 30.5 us
  Pallas kernels  29.2 us (95%)
  between operations  0.64 us (2%)
  local copies, waits for them, and re-layouts  0.61 us (2%)
    pallas_call x1, Pallas kernels, local(): pl.pallas_call(kernel, out_shape=pltpu.VMEM((2, CD, DOF), f32), in_specs=...  29.2 us

profile of v7, /device:TPU:6, one launch (start us, length us, event | category | flops | bytes accessed | tf_op | source)
XLA Modules:
  0.0 30.5 jit_solution(7574555079251588528)
XLA Ops:
  0.6 29.2 %shard_map.113 = f32[2,4,512]{2,1,0:T(4,128)S(1)} custom-call(f32[4,512]{1,0:T(4,128)} %u_hbm.1, f32[4,512]{1,0:T(4,128)} %load_hbm.1, f32[1,512]{1,0:T(1,128)} %bitcast.6, s32[2,4]{1,0:T(2,128)} %bitcast.7, s32[1,512]{1,0:T(1,128)} %dofs_hbm.1, s32[1,256]{1,0:T(1,128)} %owner_hbm.1, bf16[4,128,128]{2,1,0:T(8,128)(2,1)} %constant.2.clone.basis_hbm, ...), custom_call_target="tpu_custom_call" | custom-call | tf_op jit(solution)/shard_map/pallas_call | solution.py:530
  29.9 0.6 %slice_bitcast_fusion = (f32[4,512]{1,0:T(4,128)}, f32[4,512]{1,0:T(4,128)}) fusion(f32[2,4,512]{2,1,0:T(4,128)S(1)} %shard_map.113), kind=kLoop, calls=%fused_computation | loop fusion | bytes 32768 | tf_op jit(solution)/shard_map/squeeze | solution.py:579
